TPU v7x, 256 devices: a whole 4x4x8 slice. The times are simulated.
256 devices in a mesh: rows: 64 (over x, z_hi, y), grp: 4 (over z_lo, core).
Axes of the slice: x: 4, y: 4, z: 8 (z_hi: 4, z_lo: 2; z = z_hi * 2 + z_lo), core: 2. Of those that a mesh axis runs over, the one named last changes fastest.
Arguments:
- single: bfloat16 [768, 384], P('grp'), may hold values from -6 to 6
- pair: bfloat16 [768, 768, 128], P('rows', 'grp'), may hold values from -6 to 6
- chains: int32 [768], replicated, may hold values from 0 to 3, as said below
- noised: bfloat16 [64, 768, 768], P('rows', 'grp'), may hold values from -6 to 6
- w_gamma: bfloat16 [384, 768], replicated, may hold values from -0.3125 to 0.3125
- w_beta: bfloat16 [384, 768], replicated, may hold values from -0.3125 to 0.3125
- w_outgate: bfloat16 [384, 768], replicated, may hold values from -0.3125 to 0.3125
- w_query: bfloat16 [768, 768], replicated, may hold values from -0.21875 to 0.21875
- w_key: bfloat16 [768, 768], replicated, may hold values from -0.21875 to 0.21875
- w_value: bfloat16 [768, 768], replicated, may hold values from -0.21875 to 0.21875
- w_out: bfloat16 [768, 768], replicated, may hold values from -0.21875 to 0.21875
- w_pair: bfloat16 [128, 16], replicated, may hold values from -0.5 to 0.5
- chain_gain: float32 [16], replicated, may hold values from -3 to 6
- cotangent: bfloat16 [64, 768, 768], P('rows', 'grp'), may hold values from -6 to 6
Outputs:
- updated: bfloat16 [64, 768, 768], P('rows', 'grp')
- d_single: float32 [768, 384], P('grp')
- d_pair: bfloat16 [768, 768, 128], P('rows', 'grp')
Inputs may be any that keep to these rules, and one draw needn't show every extreme that they name: `chains`: chain numbers never fall along the tokens; each chain has 1 to 384 tokens, one exactly 384.
All inputs are finite; a program needn't handle non-finite values.
Results may differ from a plain program's by a relative error of at most 0.022.
Values may be sent and summed in bfloat16 or wider, within the bound.
A program may use at most 128 MiB of HBM per device.

v0:
```python
import math

import jax
import jax.numpy as jnp
from jax import lax
from jax.sharding import PartitionSpec as P

EPSILON = 1e-05


def norm_rows(values):
    center = values - jnp.mean(values, axis=-1, keepdims=True)
    inverse = lax.rsqrt(jnp.mean(center * center, axis=-1, keepdims=True) + EPSILON)
    return (center * inverse, inverse)


def norm_back(grad_in, normed, inverse):
    grad_mean = jnp.mean(grad_in, axis=-1, keepdims=True)
    cross_mean = jnp.mean(grad_in * normed, axis=-1, keepdims=True)
    return inverse * (grad_in - grad_mean - normed * cross_mean)


def project(acts, weight):
    return jnp.einsum("std,de->ste", acts, weight, preferred_element_type=jnp.float32)


def project_back(acts, weight):
    return jnp.einsum("ste,de->std", acts, weight, preferred_element_type=jnp.float32)


def on_device(
    single,
    pair,
    chains,
    noised,
    w_gamma,
    w_beta,
    w_outgate,
    w_query,
    w_key,
    w_value,
    w_out,
    w_pair,
    chain_gain,
    cotangent,
):
    col_count = single.shape[0]
    row_count = pair.shape[0]
    head_count = w_pair.shape[1]
    model_width = w_query.shape[0]
    head_size = model_width // head_count
    sample_count = noised.shape[0]
    token_total = chains.shape[0]
    score_scale = 1.0 / math.sqrt(head_size)
    row_index = lax.axis_index("rows")
    group_index = lax.axis_index("grp")
    chain_rows = lax.dynamic_slice_in_dim(chains, row_index * row_count, row_count)
    chain_cols = lax.dynamic_slice_in_dim(chains, group_index * col_count, col_count)
    pair_norm, pair_inv = norm_rows(pair.astype(jnp.float32))
    projected = jnp.einsum(
        "ijc,ch->hij", pair_norm.astype(jnp.bfloat16), w_pair, preferred_element_type=jnp.float32
    )
    same_chain = (chain_rows[:, None] == chain_cols[None, :]).astype(jnp.float32)
    bias_block = (projected + chain_gain[:, None, None] * same_chain[None]).astype(jnp.bfloat16)
    bias_keys = lax.all_gather(bias_block, "rows", axis=1, tiled=True)
    single_norm, single_inv = norm_rows(single.astype(jnp.float32))
    single_b = single_norm.astype(jnp.bfloat16)
    cond_gamma = jax.nn.sigmoid(jnp.dot(single_b, w_gamma, preferred_element_type=jnp.float32))
    cond_beta = jnp.dot(single_b, w_beta, preferred_element_type=jnp.float32)
    out_gate = jax.nn.sigmoid(jnp.dot(single_b, w_outgate, preferred_element_type=jnp.float32))
    noised_f = noised.astype(jnp.float32)
    noised_norm, noised_inv = norm_rows(noised_f)
    x_b = (noised_norm * cond_gamma[None] + cond_beta[None]).astype(jnp.bfloat16)
    queries = project(x_b, w_query).astype(jnp.bfloat16)
    keys_own = project(x_b, w_key).astype(jnp.bfloat16)
    values_own = project(x_b, w_value).astype(jnp.bfloat16)
    queries_all = lax.all_gather(queries, "grp", axis=1, tiled=True)
    query_heads = queries_all.reshape(sample_count, token_total, head_count, head_size)
    key_heads = keys_own.reshape(sample_count, col_count, head_count, head_size)
    value_heads = values_own.reshape(sample_count, col_count, head_count, head_size)
    scores = (
        jnp.einsum("sihe,sjhe->shij", query_heads, key_heads, preferred_element_type=jnp.float32)
        * score_scale
        + bias_keys.astype(jnp.float32)[None]
    )
    exp_scores = jnp.exp(scores)
    exp_total = lax.psum(jnp.sum(exp_scores, axis=-1).astype(jnp.bfloat16), "grp").astype(
        jnp.float32
    )
    attn_prob = exp_scores / exp_total[..., None]
    prob_b = attn_prob.astype(jnp.bfloat16)
    attended_part = jnp.einsum(
        "shij,sjhe->sihe", prob_b, value_heads, preferred_element_type=jnp.float32
    )
    attended_part = attended_part.reshape(sample_count, token_total, model_width)
    attended = lax.psum_scatter(
        attended_part.astype(jnp.bfloat16), "grp", scatter_dimension=1, tiled=True
    )
    block_update = project(attended, w_out)
    updated = (noised_f + out_gate[None] * block_update).astype(jnp.bfloat16)
    grad_out = cotangent.astype(jnp.float32)
    gate_part = jnp.sum(grad_out * block_update, axis=0)
    grad_update = (grad_out * out_gate[None]).astype(jnp.bfloat16)
    grad_attn = project_back(grad_update, w_out).astype(jnp.bfloat16)
    grads_all = lax.all_gather(grad_attn, "grp", axis=1, tiled=True)
    grad_heads = grads_all.reshape(sample_count, token_total, head_count, head_size)
    grad_prob = jnp.einsum(
        "sihe,sjhe->shij", grad_heads, value_heads, preferred_element_type=jnp.float32
    )
    row_delta = lax.psum(
        jnp.sum(attn_prob * grad_prob, axis=-1).astype(jnp.bfloat16), "grp"
    ).astype(jnp.float32)
    grad_score = attn_prob * (grad_prob - row_delta[..., None])
    score_b = grad_score.astype(jnp.bfloat16)
    query_part = (
        jnp.einsum("shij,sjhe->sihe", score_b, key_heads, preferred_element_type=jnp.float32)
        * score_scale
    )
    query_part = query_part.reshape(sample_count, token_total, model_width)
    grad_query = lax.psum_scatter(
        query_part.astype(jnp.bfloat16), "grp", scatter_dimension=1, tiled=True
    )
    grad_key = (
        jnp.einsum("shij,sihe->sjhe", score_b, query_heads, preferred_element_type=jnp.float32)
        * score_scale
    )
    grad_value = jnp.einsum(
        "shij,sihe->sjhe", prob_b, grad_heads, preferred_element_type=jnp.float32
    )
    grad_key = grad_key.reshape(sample_count, col_count, model_width).astype(jnp.bfloat16)
    grad_value = grad_value.reshape(sample_count, col_count, model_width).astype(jnp.bfloat16)
    grad_input = (
        project_back(grad_query, w_query)
        + project_back(grad_key, w_key)
        + project_back(grad_value, w_value)
    )
    gamma_part = jnp.sum(grad_input * noised_norm, axis=0)
    beta_part = jnp.sum(grad_input, axis=0)
    gamma_sum, beta_sum, gate_sum = lax.psum((gamma_part, beta_part, gate_part), "rows")
    pre_gamma = (gamma_sum * cond_gamma * (1.0 - cond_gamma)).astype(jnp.bfloat16)
    pre_gate = (gate_sum * out_gate * (1.0 - out_gate)).astype(jnp.bfloat16)
    grad_snorm = jnp.dot(pre_gamma, w_gamma.T, preferred_element_type=jnp.float32)
    grad_snorm = grad_snorm + jnp.dot(
        beta_sum.astype(jnp.bfloat16), w_beta.T, preferred_element_type=jnp.float32
    )
    grad_snorm = grad_snorm + jnp.dot(pre_gate, w_outgate.T, preferred_element_type=jnp.float32)
    d_single = norm_back(grad_snorm, single_norm, single_inv)
    bias_part = jnp.sum(score_b, axis=0, dtype=jnp.float32)
    bias_own = lax.psum_scatter(bias_part, "rows", scatter_dimension=1, tiled=True)
    bias_grad = (bias_own * token_total).astype(jnp.bfloat16)
    grad_pairn = jnp.einsum("hij,ch->ijc", bias_grad, w_pair, preferred_element_type=jnp.float32)
    d_pair = norm_back(grad_pairn, pair_norm, pair_inv).astype(jnp.bfloat16)
    return (updated, d_single, d_pair)


def solution(mesh):
    in_specs = (
        P("grp", None),
        P("rows", "grp", None),
        P(),
        P("rows", "grp", None),
        P(),
        P(),
        P(),
        P(),
        P(),
        P(),
        P(),
        P(),
        P(),
        P("rows", "grp", None),
    )
    out_specs = (P("rows", "grp", None), P("grp", None), P("rows", "grp", None))
    return jax.shard_map(
        on_device, mesh=mesh, in_specs=in_specs, out_specs=out_specs, check_vma=False
    )
```

profile of v0, /device:TPU:2, one launch (start us, length us, event | category | flops | bytes accessed | tf_op | source)
XLA Modules:
  0.0 1301.3 jit_solution(7301593065374131071)
XLA Ops:
  23.6 1.7 convolution_convert_fusion.1
  26.2 1.7 convolution_convert_fusion.3
  28.8 13.2 %all-gather.10.cloned.1.call-done = bf16[768,768]{1,0:T(8,128)(2,1)} async-done(((bf16[192,768]{1,0:T(8,128)(2,1)}), bf16[768,768]{1,0:T(8,128)(2,1)}) %all-gather.10.cloned.1.call-update) | async-done | bytes 1179664 | tf_op jit(solution)/shard_map/all_gather | solution.py:105
  42.0 2.4 copy.37
  44.4 24.8 %all-gather.8.cloned.1.call-done = bf16[768,768]{1,0:T(8,128)(2,1)} async-done(((bf16[192,768]{1,0:T(8,128)(2,1)}), bf16[768,768]{1,0:T(8,128)(2,1)}) %all-gather.8.cloned.1.call-update) | async-done | bytes 1179664 | tf_op jit(solution)/shard_map/all_gather | solution.py:77
  70.8 102.8 %all-gather.6.cloned.1.call-done = bf16[16,768,192]{2,0,1:T(8,128)(2,1)} async-done(((bf16[16,12,192]{2,0,1:T(8,128)(2,1)}), bf16[16,768,192]{2,0,1:T(8,128)(2,1)}) %all-gather.6.cloned.1.call-update) | async-done | bytes 4718608 | tf_op jit(solution)/shard_map/all_gather | solution.py:65
  173.5 8.7 copy.36
  182.2 7.3 fusion.1
  189.6 13.2 %psum.35 = bf16[16,768]{1,0:T(8,128)(2,1)} all-reduce(bf16[16,768]{1,0:T(8,128)(2,1)} %get-tuple-element.14), channel_id=1, replica_groups=mesh['rows'=64,'grp'=4] {'grp'}, use_global_device_ids=true, to_apply=%region_7.0 | all-reduce | flops 12288 | bytes 49152 | tf_op jit(solution)/shard_map/psum | solution.py:87
  203.4 15.3 %multiply_reduce_fusion = (bf16[16,768]{1,0:T(8,128)(2,1)}, f32[16,768,192]{1,2,0:T(8,128)}, f32[16,768,192]{1,2,0:T(8,128)}) fusion(f32[16,768]{1,0:T(8,128)S(1)} %div.58, bf16[16,768,192]{1,2,0:T(8,128)(2,1)} %copy.36, f32[16,768,192]{1,2,0:T(8,128)} %get-tuple-element.15, bf16[768,16,48]{0,2,1:T(8,128)(2,1)} %bitcast.127, bf16[192,16,48]{0,2,1:T(8,128)(2,1)} %bitcast.131), kind=kOutput, calls=%fused_computation.1 | convolution fusion | flops 240635904 | bytes 34578432 | tf_op jit(solution)/shard_map/sihe,sjhe->shij/dot_general | solution.py:107
  218.7 11.6 psum.36
  231.6 10.2 multiply_convert_fusion
  241.9 4.4 multiply_convert_fusion.1
  246.3 6.7 copy.41
  253.0 2.9 copy.47
  256.0 5.8 fusion.6
  261.8 6.7 copy.39
  268.5 2.9 copy.48
  271.5 4.8 fusion.14
  276.3 6.1 fusion.15
  282.4 2.2 reshape_bitcast_fusion
  284.6 2.0 copy.42
  290.2 13.9 %reduce-scatter.10.cloned.1.call-done = bf16[192,768]{1,0:T(8,128)(2,1)} async-done(((bf16[768,768]{1,0:T(8,128)(2,1)}), bf16[192,768]{1,0:T(8,128)(2,1)}) %reduce-scatter.10.cloned.1.call-update) | async-done | bytes 294928
  304.1 2.1 reshape_bitcast_fusion.1
  306.2 2.0 copy.40
  308.2 2.6 fusion.41
  310.9 10.0 copy.38
  320.9 345.6 %all-reduce.5 = bf16[192,768]{1,0:T(8,128)(2,1)} all-reduce(f32[192,768]{1,0:T(8,128)S(1)} %convolution_add_fusion), channel_id=1, replica_groups=mesh['rows'=64,'grp'=4] {'rows'}, use_global_device_ids=true, to_apply=%region_13.0 | all-reduce | flops 147456 | bytes 884736 | tf_op jit(solution)/shard_map/psum | solution.py:139
  666.5 333.2 %all-reduce.4.cloned.1.call-done = (f32[192,768]{1,0:T(8,128)}, f32[192,768]{1,0:T(8,128)}) async-done(((f32[192,768]{1,0:T(8,128)}, f32[192,768]{1,0:T(8,128)}), (f32[192,768]{1,0:T(8,128)}, f32[192,768]{1,0:T(8,128)})) %all-reduce.4.cloned.1.call-update) | async-done | bytes 1179664 | tf_op jit(solution)/shard_map/psum | solution.py:139
  1004.2 284.8 %reduce-scatter.8.cloned.1.call-done = f32[16,12,192]{2,0,1:T(8,128)} async-done(((f32[16,768,192]{2,0,1:T(8,128)}), f32[16,12,192]{2,0,1:T(8,128)}) %reduce-scatter.8.cloned.1.call-update) | async-done | bytes 147472 | tf_op jit(solution)/shard_map/reduce_scatter | solution.py:149
  1289.1 3.1 fusion.75
  1292.2 2.3 fusion.29
  (117 shorter events, 29.8 us)
Async XLA Ops:
  7.2 6.3 copy-start
  7.2 34.9 %all-gather.10.cloned.1.call-start = ((), (), s32[]{:S(2)}) async-start(), calls=%async_computation.6 | async-start | bytes 1474560 | tf_op jit(solution)/shard_map/all_gather | solution.py:105
  8.4 8.0 copy-start.28
  10.6 5.8 copy-start.24
  11.8 4.7 copy-start.26
  11.8 4.7 copy-start.29
  11.8 1.6 copy-start.17
  13.4 1.4 copy-start.9
  14.8 1.7 copy-start.4
  14.8 1.7 copy-start.11
  14.8 54.4 %all-gather.8.cloned.1.call-start = ((), (), s32[]{:S(2)}) async-start(), calls=%async_computation.5 | async-start | bytes 1474560 | tf_op jit(solution)/shard_map/all_gather | solution.py:77
  16.4 1.5 copy-start.2
  17.9 2.7 copy-start.1
  19.0 2.8 copy-start.30
  19.0 2.8 copy-start.32
  19.0 154.5 %all-gather.6.cloned.1.call-start = ((), (), s32[]{:S(2)}) async-start(), calls=%async_computation.3 | async-start | bytes 6389760 | tf_op jit(solution)/shard_map/all_gather | solution.py:65
  21.9 3.4 copy-start.22
  23.5 258.9 %reduce-scatter.12.cloned.1.call-start = ((), (), s32[]{:S(2)}) async-start(), calls=%async_computation.8 | async-start | bytes 1474560
  255.9 48.2 %reduce-scatter.10.cloned.1.call-start = ((), (), s32[]{:S(2)}) async-start(), calls=%async_computation.7 | async-start | bytes 1474560
  271.5 728.3 %all-reduce.4.cloned.1.call-start = ((), (), s32[]{:S(2)}) async-start(), calls=%async_computation.9 | async-start | bytes 2359296 | tf_op jit(solution)/shard_map/psum | solution.py:139
  271.5 4.8 copy-start.8
  282.4 4.2 copy-start.3
  286.6 1.7 copy-start.6
  286.6 1.7 copy-start.16
  290.2 18.0 %copy-start.5 = (bf16[1,192,768]{2,1,0:T(8,128)(2,1)S(1)}, bf16[1,192,768]{2,1,0:T(8,128)(2,1)}, u32[]{:S(2)}) copy-start(bf16[1,192,768]{2,1,0:T(8,128)(2,1)} %param.17) | copy-start | bytes 884740
  290.2 18.0 %copy-start.18 = (bf16[1,192,768]{2,1,0:T(8,128)(2,1)S(1)}, bf16[1,192,768]{2,1,0:T(8,128)(2,1)}, u32[]{:S(2)}) copy-start(bf16[1,192,768]{2,1,0:T(8,128)(2,1)} %param.27) | copy-start | bytes 884740
  310.9 978.2 %reduce-scatter.8.cloned.1.call-start = ((), (), s32[]{:S(2)}) async-start(), calls=%async_computation.4 | async-start | bytes 12779520 | tf_op jit(solution)/shard_map/reduce_scatter | solution.py:149
  320.9 678.9 %copy-start.14 = (f32[192,768]{1,0:T(8,128)S(1)}, f32[192,768]{1,0:T(8,128)}, u32[]{:S(2)}) copy-start(f32[192,768]{1,0:T(8,128)} %copy-done.13) | copy-start | bytes 1769476
  666.5 334.9 %copy-start.12 = (bf16[384,768]{1,0:T(8,128)(2,1)S(1)}, bf16[384,768]{1,0:T(8,128)(2,1)}, u32[]{:S(2)}) copy-start(bf16[384,768]{1,0:T(8,128)(2,1)} %param.19) | copy-start | bytes 1769476
  999.7 1.7 copy-start.19
  1002.8 286.3 %copy-start.23 = (f32[12,192]{1,0:T(8,128)S(1)}, f32[12,192]{1,0:T(8,128)}, u32[]{:S(2)}) copy-start(f32[12,192]{1,0:T(8,128)} %copy-done.22) | copy-start | bytes 27652
  1002.8 286.3 %copy-start.31 = (bf16[128,16]{0,1:T(8,128)(2,1)S(1)}, bf16[128,16]{0,1:T(8,128)(2,1)}, u32[]{:S(2)}) copy-start(bf16[128,16]{0,1:T(8,128)(2,1)} %param.25) | copy-start | bytes 12292
  (8 other events, 9.4 us)
Sparse Core Ops, SparseCore 0:
  14.9 27.1 all-gather.9
  44.4 24.7 all-gather.7
  72.5 101.0 all-gather.5
  256.0 21.3 reduce-scatter.11
  279.9 24.1 reduce-scatter.9
  311.0 688.7 all-reduce.3
  1005.6 283.4 reduce-scatter.7
where the time goes:
time: 1300 us
  waiting for transfers between devices  773 us (59%)
  blocking collectives  370 us (28%)
  matrix products  65.6 us (5%)
  local copies, waits for them, and re-layouts  56.3 us (4%)
  other arithmetic  21.3 us (2%)
  between operations  14.6 us (1%)
    psum x1, blocking collectives, on_device(): lax.psum((gamma_part, beta_part, gate_part), 'rows')  346 us
    psum x1, waiting for transfers between devices, on_device(): lax.psum((gamma_part, beta_part, gate_part), 'rows')  333 us
    reduce_scatter x1, waiting for transfers between devices, on_device(): lax.psum_scatter(bias_part, 'rows', scatter_dimension=1, tiled=True)  285 us
    all_gather x1, waiting for transfers between devices, on_device(): bias_keys = lax.all_gather(bias_block, 'rows', axis=1, tiled=True)  103 us
    unnamed x74, local copies, waits for them, and re-layouts  30.3 us
  transfers between devices with their start and end apart: 7, of which 6 were waited for; matrix products, arithmetic and copies ran while one was open for 5% of the time, Pallas kernels for 0%

commit v1 on v0

v1 whole, which is shorter than its diff:
```python
import math

import jax
import jax.numpy as jnp
from jax import lax
from jax.experimental import pallas as pl
from jax.experimental.pallas import tpu as pltpu
from jax.sharding import PartitionSpec as P

EPSILON = 1e-05
LOG2E = math.log2(math.e)
F32 = jnp.float32
BF16 = jnp.bfloat16
MESH = pl.DeviceIdType.MESH
ANY = pl.BlockSpec(memory_space=pl.ANY)
VMEM = pl.BlockSpec(memory_space=pltpu.VMEM)
SMEM = pl.BlockSpec(memory_space=pltpu.SMEM)
VMEM_BYTES = 56 * 1024 * 1024

HEADS = 16
HEAD = 48
WIDTH = 768
TOKENS = 768
BLOCK = 192
ROWS = 12
CHUNK = 6 * HEAD


def dot(left, right, contract=((1,), (0,))):
    return lax.dot_general(left, right, (contract, ((), ())), preferred_element_type=F32)


def norm_rows(values):
    center = values - jnp.mean(values, axis=-1, keepdims=True)
    inverse = lax.rsqrt(jnp.mean(center * center, axis=-1, keepdims=True) + EPSILON)
    return center * inverse, inverse


def norm_back(grad_in, normed, inverse):
    grad_mean = jnp.mean(grad_in, axis=-1, keepdims=True)
    cross_mean = jnp.mean(grad_in * normed, axis=-1, keepdims=True)
    return inverse * (grad_in - grad_mean - normed * cross_mean)


def iota(shape, dim):
    return lax.broadcasted_iota(jnp.int32, shape, dim)


def front_kernel(
    single,
    pair,
    chain_all,
    chain_cols,
    noised,
    w_gamma,
    w_beta,
    w_outgate,
    w_query,
    w_key,
    w_value,
    w_out,
    w_pair,
    chain_gain,
    cotangent,
    bias_out,
    acts_out,
    gamma_out,
    gate_out,
):
    row_index = lax.axis_index("rows")
    group_index = lax.axis_index("grp")
    cols = chain_cols[pl.ds(group_index, 1), :]
    w_pair_t = w_pair[...].astype(F32).T.astype(BF16)
    gain = chain_gain[...]
    strips = []
    for i in range(ROWS):
        normed, _ = norm_rows(pair[i].astype(F32))
        projected = dot(w_pair_t, normed.astype(BF16), ((1,), (1,)))
        same = (cols == chain_all[row_index * ROWS + i]).astype(F32)
        strips.append((projected + gain * same).astype(BF16))
    strips = jnp.concatenate(strips, axis=0)
    shape = (HEADS * 16, HEADS * ROWS)
    to, source = iota(shape, 0), iota(shape, 1)
    order = ((to // 16 == source % 16) & (to % 16 == source // 16)).astype(BF16)
    bias_out[:, :BLOCK] = dot(order, strips).astype(BF16)
    bias_out[:, BLOCK:] = jnp.zeros((HEADS * 16, 256 - BLOCK), BF16)

    single_norm, _ = norm_rows(single[...].astype(F32))
    single_b = single_norm.astype(BF16)
    gamma = jax.nn.sigmoid(dot(single_b, w_gamma[...]))
    beta = dot(single_b, w_beta[...])
    gate = jax.nn.sigmoid(dot(single_b, w_outgate[...]))
    gamma_out[...] = gamma
    gate_out[...] = gate
    noised_norm, _ = norm_rows(noised[...].astype(F32))
    x_b = (noised_norm * gamma + beta).astype(BF16)
    grad_update = (cotangent[...].astype(F32) * gate).astype(BF16)
    arrays = [
        dot(x_b, w_query[...]),
        dot(x_b, w_key[...]),
        dot(x_b, w_value[...]),
        dot(grad_update, w_out[...], ((1,), (1,))),
    ]
    pieces = [a[:128].T.astype(BF16) for a in arrays]
    for first, second in ((0, 2), (1, 3)):
        tail = jnp.concatenate([arrays[first][128:], arrays[second][128:]], axis=0)
        pieces.append(tail.T.astype(BF16))
    for h in range(HEADS):
        for n, piece in enumerate(pieces):
            acts_out[h * CHUNK + n * HEAD : h * CHUNK + (n + 1) * HEAD, :] = piece[
                h * HEAD : (h + 1) * HEAD
            ]


class Place:
    def __init__(self):
        self.r = lax.axis_index("rows")
        self.b = lax.axis_index("grp")
        self.x = self.r // 16
        self.z = (self.r // 4) % 4
        self.y = self.r % 4
        self.me = self.y * 4 + self.b

    def group(self, k):
        peer = (self.me + k) % 16
        return peer, (self.r - self.y + peer // 4, peer % 4)

    def group_from(self, k):
        return (self.me + 16 - k) % 16

    def along(self, axis, k):
        if axis == "x":
            place = (self.x + k) % 4
            return place, (self.r + (place - self.x) * 16, self.b)
        if axis == "z":
            place = (self.z + k) % 4
            return place, (self.r + (place - self.z) * 4, self.b)
        place = (self.y + k) % 4
        return place, (self.r + (place - self.y), self.b)

    def along_from(self, axis, k):
        return ({"x": self.x, "z": self.z, "y": self.y}[axis] + 4 - k) % 4


def remote(source, target, send, recv, device):
    return pltpu.make_async_remote_copy(
        src_ref=source,
        dst_ref=target,
        send_sem=send,
        recv_sem=recv,
        device_id=device,
        device_id_type=MESH,
    )


def enter(devices):
    barrier = pltpu.get_barrier_semaphore()
    for device in devices:
        pl.semaphore_signal(barrier, inc=1, device_id=device, device_id_type=MESH)
    pl.semaphore_wait(barrier, len(devices))


def gather_kernel(
    bias_in, acts_in, acts_all, bias_all, held, mine, a_send, a_recv, b_send, b_recv, s_send, s_recv, local
):
    at = Place()
    enter(
        [at.group(k)[1] for k in range(1, 16)]
        + [at.along("z", k)[1] for k in range(1, 4)]
        + [at.along("x", k)[1] for k in range(1, 4)]
    )
    out = []
    for k in range(1, 16):
        peer, device = at.group(k)
        copy = remote(bias_in.at[peer], held.at[at.me], b_send.at[k], b_recv.at[k], device)
        copy.start()
        out.append(copy)
    own_bias = pltpu.make_async_copy(bias_in.at[at.me], held.at[at.me], local.at[0])
    own_bias.start()
    for k in range(1, 16):
        peer, device = at.group(k)
        copy = remote(acts_in.at[peer], acts_all.at[at.me], a_send.at[k], a_recv.at[k], device)
        copy.start()
        out.append(copy)
    own_acts = pltpu.make_async_copy(acts_in.at[at.me], acts_all.at[at.me], local.at[1])
    own_acts.start()

    own_bias.wait()
    for k in range(1, 16):
        source = at.group_from(k)
        remote(
            bias_in.at[source], held.at[source], b_send.at[k], b_recv.at[k], at.group(k)[1]
        ).wait_recv()
    strips = []
    for y in range(4):
        parts = [held[y * 4 + b] for b in range(4)]
        tails = [p[:, 128:BLOCK] for p in parts]
        strips.append(jnp.concatenate([p[:, :128] for p in parts] + tails, axis=1))
    strips = jnp.concatenate(strips, axis=0)
    to, source = iota((HEAD, 64), 0), iota((HEAD, 64), 1)
    pick = ((source // 16 == to // ROWS) & (source % 16 == to % ROWS)).astype(BF16)
    mine[...] = dot(pick, strips).astype(BF16)
    own_rows = pltpu.make_async_copy(mine, bias_all.at[at.x, at.z], local.at[2])
    own_rows.start()
    for k in range(1, 4):
        _, device = at.along("z", k)
        copy = remote(mine, bias_all.at[at.x, at.z], s_send.at[k], s_recv.at[k], device)
        copy.start()
        out.append(copy)
    own_rows.wait()
    for k in range(1, 4):
        source = at.along_from("z", k)
        remote(
            mine, bias_all.at[at.x, source], s_send.at[k], s_recv.at[k], at.along("z", k)[1]
        ).wait_recv()
    for k in range(1, 4):
        _, device = at.along("x", k)
        copy = remote(bias_all.at[at.x], bias_all.at[at.x], s_send.at[4 + k], s_recv.at[4 + k], device)
        copy.start()
        out.append(copy)
    for k in range(1, 4):
        source = at.along_from("x", k)
        remote(
            bias_all.at[source],
            bias_all.at[source],
            s_send.at[4 + k],
            s_recv.at[4 + k],
            at.along("x", k)[1],
        ).wait_recv()
    own_acts.wait()
    for k in range(1, 16):
        source = at.group_from(k)
        remote(
            acts_in.at[source], acts_all.at[source], a_send.at[k], a_recv.at[k], at.group(k)[1]
        ).wait_recv()
    for copy in out:
        copy.wait_send()


def scatter_kernel(
    grads_in, bias_in, grads_all, bias_out, from_x, to_z, from_z, to_group,
    a_send, a_recv, b_send, b_recv, s_send, s_recv, local,
):
    at = Place()
    enter(
        [at.group(k)[1] for k in range(1, 16)]
        + [at.along("z", k)[1] for k in range(1, 4)]
        + [at.along("x", k)[1] for k in range(1, 4)]
    )
    out = []
    for k in range(1, 4):
        place, device = at.along("x", k)
        copy = remote(bias_in.at[place], from_x.at[at.x], s_send.at[k], s_recv.at[k], device)
        copy.start()
        out.append(copy)
    own_bias = pltpu.make_async_copy(bias_in.at[at.x], from_x.at[at.x], local.at[0])
    own_bias.start()
    for k in range(1, 16):
        peer, device = at.group(k)
        copy = remote(grads_in.at[peer], grads_all.at[at.me], a_send.at[k], a_recv.at[k], device)
        copy.start()
        out.append(copy)
    own_acts = pltpu.make_async_copy(grads_in.at[at.me], grads_all.at[at.me], local.at[1])
    own_acts.start()

    own_bias.wait()
    for k in range(1, 4):
        source = at.along_from("x", k)
        remote(
            bias_in.at[source], from_x.at[source], s_send.at[k], s_recv.at[k], at.along("x", k)[1]
        ).wait_recv()
    for z in range(4):
        rows = slice(z * HEAD, (z + 1) * HEAD)
        total = from_x[0, rows, :].astype(F32)
        for x in range(1, 4):
            total = total + from_x[x, rows, :].astype(F32)
        to_z[z] = total.astype(BF16)
    for k in range(1, 4):
        place, device = at.along("z", k)
        copy = remote(to_z.at[place], from_z.at[at.z], s_send.at[4 + k], s_recv.at[4 + k], device)
        copy.start()
        out.append(copy)
    own_rows = pltpu.make_async_copy(to_z.at[at.z], from_z.at[at.z], local.at[2])
    own_rows.start()
    own_rows.wait()
    for k in range(1, 4):
        source = at.along_from("z", k)
        remote(
            to_z.at[source], from_z.at[source], s_send.at[4 + k], s_recv.at[4 + k], at.along("z", k)[1]
        ).wait_recv()
    total = from_z[0].astype(F32)
    for z in range(1, 4):
        total = total + from_z[z].astype(F32)
    total = (total * TOKENS).astype(BF16)
    to, source = iota((64, HEAD), 0), iota((64, HEAD), 1)
    pick = ((to // 16 == source // ROWS) & (to % 16 == source % ROWS)).astype(BF16)
    spread = dot(pick, total).astype(BF16)
    for y in range(4):
        rows = spread[y * 16 : (y + 1) * 16]
        for b in range(4):
            tail = rows[:, 512 + b * 64 : 512 + (b + 1) * 64]
            to_group[y * 4 + b, :, :128] = rows[:, b * 128 : (b + 1) * 128]
            to_group[y * 4 + b, :, 128:] = jnp.concatenate([tail, jnp.zeros_like(tail)], axis=1)
    for k in range(1, 16):
        peer, device = at.group(k)
        copy = remote(to_group.at[peer], bias_out.at[at.me], b_send.at[k], b_recv.at[k], device)
        copy.start()
        out.append(copy)
    own_group = pltpu.make_async_copy(to_group.at[at.me], bias_out.at[at.me], local.at[3])
    own_group.start()
    own_acts.wait()
    for k in range(1, 16):
        source = at.group_from(k)
        remote(
            grads_in.at[source], grads_all.at[source], a_send.at[k], a_recv.at[k], at.group(k)[1]
        ).wait_recv()
    own_group.wait()
    for k in range(1, 16):
        source = at.group_from(k)
        remote(
            to_group.at[source], bias_out.at[source], b_send.at[k], b_recv.at[k], at.group(k)[1]
        ).wait_recv()
    for copy in out:
        copy.wait_send()


def reduce_kernel(part, single, result, from_y, from_z, from_x, own, send, recv):
    at = Place()
    enter([at.along(axis, k)[1] for axis in "yzx" for k in range(1, 4)])
    out = []

    def exchange(first, source, target, slot, axis):
        for k in range(1, 4):
            place, device = at.along(axis, k)
            copy = remote(source(place), target(slot), send.at[first + k], recv.at[first + k], device)
            copy.start()
            out.append(copy)
        for k in range(1, 4):
            place = at.along_from(axis, k)
            remote(
                source(slot), target(place), send.at[first + k], recv.at[first + k], at.along(axis, k)[1]
            ).wait_recv()

    def total(ref):
        value = ref[0].astype(F32)
        for n in range(1, 4):
            value = value + ref[n].astype(F32)
        return value

    from_y[pl.ds(at.y, 1)] = part[pl.ds(at.y, 1)]
    exchange(0, lambda p: part.at[p], lambda p: from_y.at[p], at.y, "y")
    from_z[pl.ds(at.z, 1)] = total(from_y).astype(BF16)[None]
    exchange(4, lambda p: from_z.at[at.z], lambda p: from_z.at[p], at.z, "z")
    from_x[pl.ds(at.x, 1)] = total(from_z).astype(BF16)[None]
    exchange(8, lambda p: from_x.at[at.x], lambda p: from_x.at[p], at.x, "x")
    normed, inverse = norm_rows(single[pl.ds(at.y, 1)][0].astype(F32))
    final = norm_back(total(from_x), normed, inverse)
    own[...] = final
    result[pl.ds(at.y, 1)] = final[None]
    exchange(12, lambda p: own, lambda p: result.at[p], at.y, "y")
    for copy in out:
        copy.wait_send()


def attention_kernel(acts, bias, grads, bias_grad, total_grad):
    sample = pl.program_id(0)
    scale = 1.0 / math.sqrt(HEAD)

    @pl.when(sample == 0)
    def _():
        total_grad[...] = jnp.zeros_like(total_grad)

    def piece(b, n):
        return acts[0, b * CHUNK + n * HEAD : b * CHUNK + (n + 1) * HEAD, :]

    def wide(n, tail, half):
        lanes = slice(half * 64, half * 64 + 64)
        parts = [piece(b, n) for b in range(4)] + [piece(b, tail)[:, lanes] for b in range(4)]
        return jnp.concatenate(parts, axis=1)

    def block(b, n, tail, half):
        lanes = slice(half * 64, half * 64 + 64)
        return jnp.concatenate([piece(b, n), piece(b, tail)[:, lanes]], axis=1)

    key_t = wide(1, 5, 0)
    value_t = wide(2, 4, 1)
    grad_key = jnp.zeros((HEAD, TOKENS), F32)
    grad_value = jnp.zeros((HEAD, TOKENS), F32)
    for b in range(4):
        rows = slice(b * BLOCK, (b + 1) * BLOCK)
        query_t = block(b, 0, 4, 0)
        grad_t = block(b, 3, 5, 1)
        query = query_t.astype(F32).T.astype(BF16)
        grad = grad_t.astype(F32).T.astype(BF16)
        scores = dot(query, key_t) * (scale * LOG2E) + bias[rows, :].astype(F32) * LOG2E
        weight = jnp.exp2(scores)
        prob = weight * (1.0 / jnp.sum(weight, axis=-1, keepdims=True))
        prob_b = prob.astype(BF16)
        grad_prob = dot(grad, value_t)
        scaled = prob * grad_prob
        grad_score = scaled - prob * jnp.sum(scaled, axis=-1, keepdims=True)
        score_b = grad_score.astype(BF16)
        total_grad[rows, :] = total_grad[rows, :] + grad_score
        attended = dot(value_t, prob_b, ((1,), (1,))).astype(BF16)
        grad_query = (dot(key_t, score_b, ((1,), (1,))) * scale).astype(BF16)
        grad_value = grad_value + dot(grad_t, prob_b)
        grad_key = grad_key + dot(query_t, score_b)
        first = b * CHUNK
        grads[0, first : first + HEAD, :] = attended[:, :128]
        grads[0, first + HEAD : first + 2 * HEAD, :] = grad_query[:, :128]
        grads[0, first + 4 * HEAD : first + 5 * HEAD, :64] = attended[:, 128:]
        grads[0, first + 5 * HEAD : first + 6 * HEAD, :64] = grad_query[:, 128:]
    grad_key = (grad_key * scale).astype(BF16)
    grad_value = grad_value.astype(BF16)
    for b in range(4):
        first = b * CHUNK
        lanes = slice(b * 128, (b + 1) * 128)
        tail = slice(512 + b * 64, 512 + (b + 1) * 64)
        grads[0, first + 2 * HEAD : first + 3 * HEAD, :] = grad_key[:, lanes]
        grads[0, first + 3 * HEAD : first + 4 * HEAD, :] = grad_value[:, lanes]
        grads[0, first + 4 * HEAD : first + 5 * HEAD, 64:] = grad_key[:, tail]
        grads[0, first + 5 * HEAD : first + 6 * HEAD, 64:] = grad_value[:, tail]

    @pl.when(sample == 3)
    def _():
        bias_grad[...] = total_grad[...].astype(BF16)


def back_kernel(
    grads, noised, cotangent, gamma_in, gate_in,
    w_gamma, w_beta, w_outgate, w_query, w_key, w_value, w_out,
    updated, part,
):
    def piece(n):
        rows = [grads[h * CHUNK + n * HEAD : h * CHUNK + (n + 1) * HEAD, :] for h in range(HEADS)]
        return jnp.concatenate(rows, axis=0).astype(F32).T.astype(BF16)

    tails = [piece(4), piece(5)]
    attended = jnp.concatenate([piece(0), tails[0][:64]], axis=0)
    grad_query = jnp.concatenate([piece(1), tails[1][:64]], axis=0)
    grad_key = jnp.concatenate([piece(2), tails[0][64:]], axis=0)
    grad_value = jnp.concatenate([piece(3), tails[1][64:]], axis=0)
    gamma = gamma_in[...]
    gate = gate_in[...]
    block_update = dot(attended, w_out[...])
    noised_f = noised[...].astype(F32)
    updated[...] = (noised_f + gate * block_update).astype(BF16)
    noised_norm, _ = norm_rows(noised_f)
    back = ((1,), (1,))
    grad_input = (
        dot(grad_query, w_query[...], back)
        + dot(grad_key, w_key[...], back)
        + dot(grad_value, w_value[...], back)
    )
    pre_gamma = (grad_input * noised_norm * (gamma * (1.0 - gamma))).astype(BF16)
    pre_gate = (cotangent[...].astype(F32) * block_update * (gate * (1.0 - gate))).astype(BF16)
    total = dot(pre_gamma, w_gamma[...], back)
    total = total + dot(grad_input.astype(BF16), w_beta[...], back)
    total = total + dot(pre_gate, w_outgate[...], back)
    part[...] = total.astype(BF16)


def pair_kernel(bias_grad, pair, w_pair, result):
    grad_t = bias_grad[...].astype(F32).T.astype(BF16)[:BLOCK]
    shape = (HEADS * 16, HEADS)
    pick = (iota(shape, 0) // 16 == iota(shape, 1)).astype(BF16)
    weight = dot(pick, w_pair[...], ((1,), (1,))).astype(BF16)
    row = iota(weight.shape, 0) % 16
    for i in range(ROWS):
        grad = dot(grad_t, jnp.where(row == i, weight, jnp.zeros_like(weight)))
        normed, inverse = norm_rows(pair[i].astype(F32))
        result[i] = norm_back(grad, normed, inverse).astype(BF16)


def on_device(
    single,
    pair,
    chains,
    noised,
    w_gamma,
    w_beta,
    w_outgate,
    w_query,
    w_key,
    w_value,
    w_out,
    w_pair,
    chain_gain,
    cotangent,
):
    noised = noised.reshape(BLOCK, WIDTH)
    cotangent = cotangent.reshape(BLOCK, WIDTH)
    local = pltpu.CompilerParams(vmem_limit_bytes=VMEM_BYTES)

    def sends(collective):
        return pltpu.CompilerParams(
            vmem_limit_bytes=VMEM_BYTES, collective_id=collective, has_side_effects=True
        )

    bias_send, acts_send, gamma, gate = pl.pallas_call(
        front_kernel,
        out_shape=[
            jax.ShapeDtypeStruct((HEADS * 16, 256), BF16),
            jax.ShapeDtypeStruct((HEADS * CHUNK, 128), BF16),
            jax.ShapeDtypeStruct((BLOCK, WIDTH), F32),
            jax.ShapeDtypeStruct((BLOCK, WIDTH), F32),
        ],
        in_specs=[VMEM, VMEM, SMEM] + [VMEM] * 12,
        out_specs=[VMEM] * 4,
        compiler_params=local,
        name="front",
    )(
        single,
        pair,
        chains,
        chains.reshape(4, BLOCK),
        noised,
        w_gamma,
        w_beta,
        w_outgate,
        w_query,
        w_key,
        w_value,
        w_out,
        w_pair,
        chain_gain.reshape(HEADS, 1),
        cotangent,
    )
    dma = pltpu.SemaphoreType.DMA
    acts_all, bias_all = pl.pallas_call(
        gather_kernel,
        out_shape=[
            jax.ShapeDtypeStruct((16, CHUNK, 128), BF16),
            jax.ShapeDtypeStruct((4, 4, HEAD, TOKENS), BF16),
        ],
        in_specs=[ANY, ANY],
        out_specs=[ANY, ANY],
        scratch_shapes=[
            pltpu.VMEM((16, 16, 256), BF16),
            pltpu.VMEM((HEAD, TOKENS), BF16),
            dma((16,)),
            dma((16,)),
            dma((16,)),
            dma((16,)),
            dma((8,)),
            dma((8,)),
            dma((3,)),
        ],
        compiler_params=sends(0),
        name="gather",
    )(bias_send.reshape(HEADS, 16, 256), acts_send.reshape(HEADS, CHUNK, 128))
    grads, bias_grad = pl.pallas_call(
        attention_kernel,
        grid=(4,),
        out_shape=[
            jax.ShapeDtypeStruct((4, 4 * CHUNK, 128), BF16),
            jax.ShapeDtypeStruct((TOKENS, TOKENS), BF16),
        ],
        in_specs=[
            pl.BlockSpec((1, 4 * CHUNK, 128), lambda s: (s, 0, 0)),
            pl.BlockSpec((TOKENS, TOKENS), lambda s: (0, 0)),
        ],
        out_specs=[
            pl.BlockSpec((1, 4 * CHUNK, 128), lambda s: (s, 0, 0)),
            pl.BlockSpec((TOKENS, TOKENS), lambda s: (0, 0)),
        ],
        scratch_shapes=[pltpu.VMEM((TOKENS, TOKENS), F32)],
        compiler_params=local,
        name="attention",
    )(acts_all.reshape(4, 4 * CHUNK, 128), bias_all.reshape(TOKENS, TOKENS))
    grads_all, bias_own = pl.pallas_call(
        scatter_kernel,
        out_shape=[
            jax.ShapeDtypeStruct((16, CHUNK, 128), BF16),
            jax.ShapeDtypeStruct((16, 16, 256), BF16),
        ],
        in_specs=[ANY, ANY],
        out_specs=[ANY, ANY],
        scratch_shapes=[
            pltpu.VMEM((4, BLOCK, TOKENS), BF16),
            pltpu.VMEM((4, HEAD, TOKENS), BF16),
            pltpu.VMEM((4, HEAD, TOKENS), BF16),
            pltpu.VMEM((16, 16, 256), BF16),
            dma((16,)),
            dma((16,)),
            dma((16,)),
            dma((16,)),
            dma((8,)),
            dma((8,)),
            dma((4,)),
        ],
        compiler_params=sends(1),
        name="scatter",
    )(grads.reshape(16, CHUNK, 128), bias_grad.reshape(4, BLOCK, TOKENS))
    updated, part = pl.pallas_call(
        back_kernel,
        out_shape=[
            jax.ShapeDtypeStruct((BLOCK, WIDTH), BF16),
            jax.ShapeDtypeStruct((BLOCK, WIDTH // 2), BF16),
        ],
        in_specs=[VMEM] * 12,
        out_specs=[VMEM] * 2,
        compiler_params=local,
        name="back",
    )(
        grads_all.reshape(16 * CHUNK, 128),
        noised,
        cotangent,
        gamma,
        gate,
        w_gamma,
        w_beta,
        w_outgate,
        w_query,
        w_key,
        w_value,
        w_out,
    )
    quarter = (4, HEAD, WIDTH // 2)
    d_single = pl.pallas_call(
        reduce_kernel,
        out_shape=jax.ShapeDtypeStruct(quarter, F32),
        in_specs=[VMEM] * 2,
        out_specs=VMEM,
        scratch_shapes=[pltpu.VMEM(quarter, BF16)] * 3
        + [pltpu.VMEM(quarter[1:], F32), dma((16,)), dma((16,))],
        compiler_params=sends(2),
        name="reduce",
    )(part.reshape(quarter), single.reshape(quarter))
    d_pair = pl.pallas_call(
        pair_kernel,
        out_shape=jax.ShapeDtypeStruct(pair.shape, BF16),
        in_specs=[VMEM] * 3,
        out_specs=VMEM,
        compiler_params=local,
        name="pair",
    )(bias_own.reshape(256, 256), pair, w_pair)
    return (
        updated.reshape(1, BLOCK, WIDTH),
        d_single.reshape(BLOCK, WIDTH // 2),
        d_pair,
    )


def solution(mesh):
    rows = P("rows", "grp", None)
    grp = P("grp", None)
    in_specs = (grp, rows, P(), rows) + (P(),) * 9 + (rows,)
    return jax.shard_map(
        on_device, mesh=mesh, in_specs=in_specs, out_specs=(rows, grp, rows), check_vma=False
    )
```

time: 1300 us -> 144 us (0.11)
  waiting for transfers between devices: 773 us -> 0 us
  blocking collectives: 370 us -> 0 us
  Pallas kernels: 0 us -> 136 us
  matrix products: 65.6 us -> 0 us
  local copies, waits for them, and re-layouts: 56.3 us -> 4.79 us
  other arithmetic: 21.3 us -> 0 us
  between operations: 14.6 us -> 0.67 us
    psum x3 -> x0, blocking collectives: 370 us -> none  [the longest x1 346 us: on_device(): lax.psum((gamma_part, beta_part, gate_part), 'rows')]
    psum x1 -> x0, waiting for transfers between devices: 333 us -> none  [on_device(): lax.psum((gamma_part, beta_part, gate_part), 'rows')]
    reduce_scatter x1 -> x0, waiting for transfers between devices: 285 us -> none  [on_device(): lax.psum_scatter(bias_part, 'rows', scatter_dimension=1, tiled=True)]
    all_gather x3 -> x0, waiting for transfers between devices: 141 us -> none  [the longest x1 103 us: on_device(): bias_keys = lax.all_gather(bias_block, 'rows', axis=1, tiled=True)]
    pallas_call x0 -> x7, Pallas kernels: none -> 136 us  [the longest x1 47.8 us: on_device(): pl.pallas_call(gather_kernel, out_shape=[jax.ShapeDtypeStruct((16, CHUNK,...]
    dot_general x22 -> x0, matrix products: 65.6 us -> none  [the longest x1 15.3 us: on_device(): jnp.einsum('sihe,sjhe->shij', grad_heads, value_heads, preferred_element_...]
    unnamed x74 -> x4, local copies, waits for them, and re-layouts: 30.3 us -> 2.1 us
    unnamed x9 -> x0, waiting for transfers between devices: 14 us -> none
  transfers between devices with their start and end apart: 7 -> 0, of which waited for: 6 -> 0; matrix products, arithmetic and copies ran while one was open for 5% -> 0% of each run, Pallas kernels for 0% -> 0%
where the time goes in v1:
time: 144 us; the launch traced here: 142 us
  Pallas kernels  136 us (94%)
  local copies, waits for them, and re-layouts  4.79 us (3%)
    pallas_call x1, Pallas kernels, on_device(): pl.pallas_call(gather_kernel, out_shape=[jax.ShapeDtypeStruct((16, CHUNK,...  47.8 us
    pallas_call x1, Pallas kernels, on_device(): pl.pallas_call(scatter_kernel, out_shape=[jax.ShapeDtypeStruct((16, CHUNK...  31.4 us
    pallas_call x1, Pallas kernels, on_device(): pl.pallas_call(reduce_kernel, out_shape=jax.ShapeDtypeStruct(quarter, F32...  24.6 us
    pallas_call x1, Pallas kernels, on_device(): pl.pallas_call(attention_kernel, grid=(4,), out_shape=[jax.ShapeDtypeStru...  13.6 us
    pallas_call x1, Pallas kernels, on_device(): pl.pallas_call(back_kernel, out_shape=[jax.ShapeDtypeStruct((BLOCK, WIDTH...  7.32 us
    pallas_call x1, Pallas kernels, on_device(): pl.pallas_call(front_kernel, out_shape=[jax.ShapeDtypeStruct((HEADS * 16,...  7.29 us
    pallas_call x1, Pallas kernels, on_device(): pl.pallas_call(pair_kernel, out_shape=jax.ShapeDtypeStruct(pair.shape, BF...  4.18 us

profile of v1, /device:TPU:2, one launch (start us, length us, event | category | flops | bytes accessed | tf_op | source)
XLA Modules:
  0.0 141.7 jit_solution(5739747065969398171)
XLA Ops:
  0.6 1.4 reshape.54.chain_cols
  2.0 1.3 copy.18.chain_gain
  3.3 1.4 copy.17.w_pair
  4.7 7.3 %front.1 = (bf16[256,256]{1,0:T(8,128)(2,1)}, bf16[4608,128]{1,0:T(8,128)(2,1)}, f32[192,768]{1,0:T(8,128)}, f32[192,768]{1,0:T(8,128)}) custom-call(bf16[192,384]{1,0:T(8,128)(2,1)} %single.1, bf16[12,192,128]{2,1,0:T(8,128)(2,1)} %pair.5, s32[768]{0:T(1024)} %chain_all.1, s32[4,192]{1,0:T(4,128)} %reshape.54.chain_cols, bf16[192,768]{1,0:T(8,128)(2,1)} %bitcast.16, ...), custom_call_target="tpu_custom_call" | custom-call | tf_op jit(solution)/shard_map/front/pallas_call | solution.py:500
  12.0 47.8 %gather.1 = (bf16[16,288,128]{2,1,0:T(8,128)(2,1)}, bf16[4,4,48,768]{3,2,1,0:T(8,128)(2,1)}) custom-call(bf16[16,16,256]{2,1,0:T(8,128)(2,1)} %bitcast.28, bf16[16,288,128]{2,1,0:T(8,128)(2,1)} %bitcast.20), custom_call_target="tpu_custom_call" | custom-call | tf_op jit(solution)/shard_map/gather/pallas_call | solution.py:530
  59.8 13.6 %attention.1 = (bf16[4,1152,128]{2,1,0:T(8,128)(2,1)}, bf16[768,768]{1,0:T(8,128)(2,1)}) custom-call(bf16[4,1152,128]{2,1,0:T(8,128)(2,1)} %bitcast.21, bf16[768,768]{1,0:T(8,128)(2,1)} %bitcast.22), custom_call_target="tpu_custom_call" | custom-call | tf_op jit(solution)/shard_map/attention/pallas_call | solution.py:552
  73.4 31.4 %scatter.1 = (bf16[16,288,128]{2,1,0:T(8,128)(2,1)}, bf16[16,16,256]{2,1,0:T(8,128)(2,1)}) custom-call(bf16[16,288,128]{2,1,0:T(8,128)(2,1)} %bitcast.23, bf16[4,192,768]{2,1,0:T(8,128)(2,1)} %bitcast.24), custom_call_target="tpu_custom_call" | custom-call | tf_op jit(solution)/shard_map/scatter/pallas_call | solution.py:571
  104.9 7.3 %back.1 = (bf16[192,768]{1,0:T(8,128)(2,1)}, bf16[192,384]{1,0:T(8,128)(2,1)}) custom-call(bf16[4608,128]{1,0:T(8,128)(2,1)} %bitcast.15, bf16[192,768]{1,0:T(8,128)(2,1)} %bitcast.17, bf16[192,768]{1,0:T(8,128)(2,1)} %bitcast.19, f32[192,768]{1,0:T(8,128)} %get-tuple-element.22.gamma_in, f32[192,768]{1,0:T(8,128)} %get-tuple-element.23.gate_in, ...), custom_call_target="tpu_custom_call" | custom-call | tf_op jit(solution)/shard_map/back/pallas_call | solution.py:595
  112.2 24.6 %reduce.1 = f32[4,48,384]{2,1,0:T(8,128)} custom-call(bf16[4,48,384]{2,1,0:T(8,128)(2,1)} %bitcast.27, bf16[4,48,384]{2,1,0:T(8,128)(2,1)} %bitcast.26), custom_call_target="tpu_custom_call" | custom-call | tf_op jit(solution)/shard_map/reduce/pallas_call | solution.py:620
  136.8 0.0 copy-start
  136.8 4.2 %pair.4 = bf16[12,192,128]{2,1,0:T(8,128)(2,1)} custom-call(bf16[256,256]{1,0:T(8,128)(2,1)} %bitcast.29, bf16[12,192,128]{2,1,0:T(8,128)(2,1)} %pair.5, bf16[128,16]{1,0:T(8,128)(2,1)} %copy.17.w_pair), custom_call_target="tpu_custom_call" | custom-call | tf_op jit(solution)/shard_map/pair/pallas_call | solution.py:630
  141.0 0.0 copy-done
  141.0 0.7 copy.21
Async XLA Ops:
  136.8 4.2 %copy-start = (f32[4,48,384]{2,1,0:T(8,128)S(1)}, f32[4,48,384]{2,1,0:T(8,128)}, u32[]{:S(2)}) copy-start(f32[4,48,384]{2,1,0:T(8,128)} %reduce.1) | copy-start | bytes 884740

commit v2 on v0

v2 whole, which is shorter than its diff:
```python
import math

import jax
import jax.numpy as jnp
from jax import lax
from jax.experimental import pallas as pl
from jax.experimental.pallas import tpu as pltpu
from jax.sharding import PartitionSpec as P

EPSILON = 1e-05
LOG2E = math.log2(math.e)
F32 = jnp.float32
BF16 = jnp.bfloat16
MESH = pl.DeviceIdType.MESH
ANY = pl.BlockSpec(memory_space=pl.ANY)
VMEM = pl.BlockSpec(memory_space=pltpu.VMEM)
SMEM = pl.BlockSpec(memory_space=pltpu.SMEM)
VMEM_BYTES = 56 * 1024 * 1024

HEADS = 16
HEAD = 48
WIDTH = 768
TOKENS = 768
BLOCK = 192
ROWS = 12
CHUNK = 6 * HEAD


def dot(left, right, contract=((1,), (0,))):
    return lax.dot_general(left, right, (contract, ((), ())), preferred_element_type=F32)


def norm_rows(values):
    center = values - jnp.mean(values, axis=-1, keepdims=True)
    inverse = lax.rsqrt(jnp.mean(center * center, axis=-1, keepdims=True) + EPSILON)
    return center * inverse, inverse


def norm_back(grad_in, normed, inverse):
    grad_mean = jnp.mean(grad_in, axis=-1, keepdims=True)
    cross_mean = jnp.mean(grad_in * normed, axis=-1, keepdims=True)
    return inverse * (grad_in - grad_mean - normed * cross_mean)


def iota(shape, dim):
    return lax.broadcasted_iota(jnp.int32, shape, dim)


class Place:
    def __init__(self):
        self.r = lax.axis_index("rows")
        self.b = lax.axis_index("grp")
        self.x = self.r // 16
        self.z = (self.r // 4) % 4
        self.y = self.r % 4
        self.me = self.y * 4 + self.b

    def group(self, k):
        peer = (self.me + k) % 16
        return peer, (self.r - self.y + peer // 4, peer % 4)

    def group_from(self, k):
        return (self.me + 16 - k) % 16

    def along(self, axis, k):
        if axis == "x":
            place = (self.x + k) % 4
            return place, (self.r + (place - self.x) * 16, self.b)
        if axis == "z":
            place = (self.z + k) % 4
            return place, (self.r + (place - self.z) * 4, self.b)
        place = (self.y + k) % 4
        return place, (self.r + (place - self.y), self.b)

    def along_from(self, axis, k):
        return ({"x": self.x, "z": self.z, "y": self.y}[axis] + 4 - k) % 4


def remote(source, target, send, recv, device):
    return pltpu.make_async_remote_copy(
        src_ref=source,
        dst_ref=target,
        send_sem=send,
        recv_sem=recv,
        device_id=device,
        device_id_type=MESH,
    )


def total_of(ref, rows=slice(None)):
    value = ref[0, rows, :].astype(F32)
    for n in range(1, 4):
        value = value + ref[n, rows, :].astype(F32)
    return value


def pair_bias(pair, chain_cols, chain_all, chain_gain, w_pair_t, at, bias_send):
    cols = chain_cols[...]
    mine = cols[:, :BLOCK]
    for b in range(1, 4):
        mine = jnp.where(at.b == b, cols[:, b * BLOCK : (b + 1) * BLOCK], mine)
    head = iota((HEADS, 1), 0)
    gain = jnp.zeros((HEADS, 1), F32)
    for h in range(HEADS):
        gain = jnp.where(head == h, chain_gain[h], gain)
    strips = []
    for i in range(ROWS):
        normed, _ = norm_rows(pair[i].astype(F32))
        projected = dot(w_pair_t[...], normed.astype(BF16), ((1,), (1,)))
        same = (mine == chain_all[at.r * ROWS + i]).astype(F32)
        strips.append((projected + gain * same).astype(BF16))
    strips = jnp.concatenate(strips, axis=0)
    shape = (HEADS * 16, HEADS * ROWS)
    to, source = iota(shape, 0), iota(shape, 1)
    order = ((to // 16 == source % 16) & (to % 16 == source // 16)).astype(BF16)
    spread = dot(order, strips).astype(BF16)
    for h in range(HEADS):
        rows = spread[h * 16 : (h + 1) * 16]
        bias_send[h, :, :128] = rows[:, :128]
        bias_send[h, :, 128:] = jnp.concatenate([rows[:, 128:], jnp.zeros((16, 64), BF16)], axis=1)


def make_acts(noised, cotangent, gamma, beta, gate, w_query, w_key, w_value, w_out, acts_send):
    noised_norm, _ = norm_rows(noised[...].astype(F32))
    x_b = (noised_norm * gamma + beta).astype(BF16)
    grad_update = (cotangent[...].astype(F32) * gate).astype(BF16)
    arrays = [
        dot(x_b, w_query[...]),
        dot(x_b, w_key[...]),
        dot(x_b, w_value[...]),
        dot(grad_update, w_out[...], ((1,), (1,))),
    ]
    pieces = [a[:128].T.astype(BF16) for a in arrays]
    for first, second in ((0, 2), (1, 3)):
        tail = jnp.concatenate([arrays[first][128:], arrays[second][128:]], axis=0)
        pieces.append(tail.T.astype(BF16))
    for h in range(HEADS):
        for n, piece in enumerate(pieces):
            acts_send[h, n * HEAD : (n + 1) * HEAD, :] = piece[h * HEAD : (h + 1) * HEAD]


def assemble_bias(held):
    strips = []
    for y in range(4):
        parts = [held[y * 4 + b] for b in range(4)]
        tails = [p[:, 128:BLOCK] for p in parts]
        strips.append(jnp.concatenate([p[:, :128] for p in parts] + tails, axis=1))
    strips = jnp.concatenate(strips, axis=0)
    to, source = iota((HEAD, 64), 0), iota((HEAD, 64), 1)
    pick = ((source // 16 == to // ROWS) & (source % 16 == to % ROWS)).astype(BF16)
    return dot(pick, strips).astype(BF16)


def spread_bias(total, to_group):
    to, source = iota((64, HEAD), 0), iota((64, HEAD), 1)
    pick = ((to // 16 == source // ROWS) & (to % 16 == source % ROWS)).astype(BF16)
    spread = dot(pick, total).astype(BF16)
    for y in range(4):
        rows = spread[y * 16 : (y + 1) * 16]
        for b in range(4):
            tail = rows[:, 512 + b * 64 : 512 + (b + 1) * 64]
            to_group[y * 4 + b, :, :128] = rows[:, b * 128 : (b + 1) * 128]
            to_group[y * 4 + b, :, 128:] = jnp.concatenate([tail, jnp.zeros_like(tail)], axis=1)


def half(n):
    return slice(n * 64, n * 64 + 64)


def wide(acts, first, n, tail, part):
    parts = [acts[first + b, n * HEAD : (n + 1) * HEAD, :] for b in range(4)]
    parts += [acts[first + b, tail * HEAD : (tail + 1) * HEAD, half(part)] for b in range(4)]
    return jnp.concatenate(parts, axis=1)


def block(acts, place, n, tail, part):
    return jnp.concatenate(
        [
            acts[place, n * HEAD : (n + 1) * HEAD, :],
            acts[place, tail * HEAD : (tail + 1) * HEAD, half(part)],
        ],
        axis=1,
    )


def attend(query_t, grad_t, key_t, value_t, bias):
    scale = 1.0 / math.sqrt(HEAD)
    query = query_t.astype(F32).T.astype(BF16)
    grad = grad_t.astype(F32).T.astype(BF16)
    scores = dot(query, key_t) * (scale * LOG2E) + bias
    weight = jnp.exp2(scores)
    prob = weight * (1.0 / jnp.sum(weight, axis=-1, keepdims=True))
    grad_prob = dot(grad, value_t)
    scaled = prob * grad_prob
    grad_score = scaled - prob * jnp.sum(scaled, axis=-1, keepdims=True)
    return prob.astype(BF16), grad_score.astype(BF16), grad_score


def back_piece(grads, n):
    rows = [grads[h, n * HEAD : (n + 1) * HEAD, :] for h in range(HEADS)]
    return jnp.concatenate(rows, axis=0).astype(F32).T.astype(BF16)


def pair_weight(w_pair_t):
    shape = (HEADS * 16, HEADS)
    pick = (iota(shape, 0) // 16 == iota(shape, 1)).astype(BF16)
    return dot(pick, w_pair_t[...]).astype(BF16)


def pair_back(grad_t, weight, pair, result, rows):
    row = iota(weight.shape, 0) % 16
    for i in rows:
        grad = dot(grad_t, jnp.where(row == i, weight, jnp.zeros_like(weight)))
        normed, inverse = norm_rows(pair[i].astype(F32))
        result[i] = norm_back(grad, normed, inverse).astype(BF16)


def block_kernel(
    single_in, pair_in, noised_in, cotangent_in,
    w_gamma_in, w_beta_in, w_outgate_in, w_query_in, w_key_in, w_value_in, w_out_in,
    chain_all, chain_cols, chain_gain, w_pair_t,
    updated, d_single, d_pair,
    single, pair, noised, cotangent, w_gamma, w_beta, w_outgate, w_query, w_key, w_value, w_out,
    bias_send, held, bias_all, acts_send, acts_all, gamma_v, gate_v,
    key_t, value_t, grad_key, grad_value, bias_f,
    to_x, from_x, to_z, from_z, to_group, from_group, grads_send, grads_all,
    part, sum_y, sum_z, sum_x, own,
    load, a_send, a_recv, b_send, b_recv, g_send, g_recv, h_send, h_recv, s_send, s_recv, r_send, r_recv,
):
    at = Place()
    barrier = pltpu.get_barrier_semaphore()
    peers = (
        [at.group(k)[1] for k in range(1, 16)]
        + [at.along("z", k)[1] for k in range(1, 4)]
        + [at.along("x", k)[1] for k in range(1, 4)]
    )
    for device in peers:
        pl.semaphore_signal(barrier, inc=1, device_id=device, device_id_type=MESH)
    loads = {}
    for n, (name, source, target) in enumerate(
        (
            ("pair", pair_in, pair),
            ("single", single_in, single),
            ("gamma", w_gamma_in, w_gamma),
            ("beta", w_beta_in, w_beta),
            ("gate", w_outgate_in, w_outgate),
            ("noised", noised_in, noised),
            ("query", w_query_in, w_query),
            ("key", w_key_in, w_key),
            ("value", w_value_in, w_value),
            ("cot", cotangent_in, cotangent),
            ("out", w_out_in, w_out),
        )
    ):
        loads[name] = pltpu.make_async_copy(source, target, load.at[n])
        loads[name].start()
    out = []

    def send(source, target, ssem, rsem, device):
        copy = remote(source, target, ssem, rsem, device)
        copy.start()
        out.append(copy)

    def arrive(buffer, ssem, rsem):
        remote(buffer, buffer, ssem, rsem, at.group(1)[1]).wait_recv()

    loads["pair"].wait()
    pair_bias(pair, chain_cols, chain_all, chain_gain, w_pair_t, at, bias_send)
    pl.semaphore_wait(barrier, len(peers))
    for k in range(1, 16):
        peer, device = at.group(k)
        send(bias_send.at[peer], held.at[at.me], b_send.at[k], b_recv.at[k], device)
    held[at.me] = bias_send[at.me]

    for name in ("single", "gamma", "beta", "gate", "noised", "query", "key", "value", "cot", "out"):
        loads[name].wait()
    single_norm, _ = norm_rows(single[...].astype(F32))
    single_b = single_norm.astype(BF16)
    gamma = jax.nn.sigmoid(dot(single_b, w_gamma[...]))
    beta = dot(single_b, w_beta[...])
    gate = jax.nn.sigmoid(dot(single_b, w_outgate[...]))
    gamma_v[...] = gamma
    gate_v[...] = gate
    make_acts(noised, cotangent, gamma, beta, gate, w_query, w_key, w_value, w_out, acts_send)

    for k in range(1, 16):
        arrive(held.at[at.group_from(k)], b_send.at[k], b_recv.at[k])
    bias_all[at.x, at.z] = assemble_bias(held)
    for k in range(1, 4):
        rows = bias_all.at[at.x, at.z]
        send(rows, rows, s_send.at[k], s_recv.at[k], at.along("z", k)[1])
    for k in range(1, 16):
        peer, device = at.group(k)
        send(acts_send.at[peer], acts_all.at[at.me], a_send.at[k], a_recv.at[k], device)
    acts_all[at.me] = acts_send[at.me]
    for k in range(1, 4):
        arrive(bias_all.at[at.x, at.along_from("z", k)], s_send.at[k], s_recv.at[k])
    for k in range(1, 4):
        rows = bias_all.at[at.x]
        send(rows, rows, s_send.at[4 + k], s_recv.at[4 + k], at.along("x", k)[1])
    for k in range(1, 16):
        arrive(acts_all.at[at.group_from(k)], a_send.at[k], a_recv.at[k])

    samples = [(at.y + 1 + s) % 4 for s in range(4)]
    for s in range(4):
        key_t[s] = wide(acts_all, samples[s] * 4, 1, 5, 0)
        value_t[s] = wide(acts_all, samples[s] * 4, 2, 4, 1)
        grad_key[s] = jnp.zeros((HEAD, TOKENS), F32)
        grad_value[s] = jnp.zeros((HEAD, TOKENS), F32)

    def step_body(step, carry):
        k = step + step // 2 - 2 * (step // 3)
        place, device = at.along("x", k)

        @pl.when(step > 0)
        def _():
            arrive(bias_all.at[place], s_send.at[8 - k], s_recv.at[8 - k])

        for z in range(4):
            bias_f[z * HEAD : (z + 1) * HEAD, :] = bias_all[place, z].astype(F32) * LOG2E
        found = []
        for s in range(4):
            slot = samples[s] * 4 + place
            query_t = block(acts_all, slot, 0, 4, 0)
            grad_t = block(acts_all, slot, 3, 5, 1)
            found.append((query_t, grad_t) + attend(query_t, grad_t, key_t[s], value_t[s], bias_f[...]))
        total = found[0][4]
        for s in range(1, 4):
            total = total + found[s][4]
        to_x[k] = total.astype(BF16)
        for s in range(4):
            query_t, grad_t, prob_b, score_b, _ = found[s]
            slot = samples[s] * 4 + place
            attended = dot(value_t[s], prob_b, ((1,), (1,))).astype(BF16)
            grad_query = dot(key_t[s], score_b, ((1,), (1,))) * (1.0 / math.sqrt(HEAD))
            grad_query = grad_query.astype(BF16)
            grad_value[s] = grad_value[s] + dot(grad_t, prob_b)
            grad_key[s] = grad_key[s] + dot(query_t, score_b)
            grads_send[slot, :HEAD, :] = attended[:, :128]
            grads_send[slot, HEAD : 2 * HEAD, :] = grad_query[:, :128]
            grads_send[slot, 4 * HEAD : 5 * HEAD, :64] = attended[:, 128:]
            grads_send[slot, 5 * HEAD :, :64] = grad_query[:, 128:]

        @pl.when(step > 0)
        def _():
            remote(to_x.at[k], from_x.at[at.x], s_send.at[8 + k], s_recv.at[8 + k], device).start()

        return carry

    lax.fori_loop(0, 4, step_body, 0)
    from_x[at.x] = to_x[0]
    for k in range(1, 4):
        out.append(
            remote(
                to_x.at[k], from_x.at[at.x], s_send.at[8 + k], s_recv.at[8 + k], at.along("x", k)[1]
            )
        )

    for s in range(4):
        key_b = (grad_key[s] * (1.0 / math.sqrt(HEAD))).astype(BF16)
        value_b = grad_value[s].astype(BF16)
        for b in range(4):
            slot = samples[s] * 4 + b
            lanes = slice(b * 128, (b + 1) * 128)
            tail = slice(512 + b * 64, 512 + (b + 1) * 64)
            grads_send[slot, 2 * HEAD : 3 * HEAD, :] = key_b[:, lanes]
            grads_send[slot, 3 * HEAD : 4 * HEAD, :] = value_b[:, lanes]
            grads_send[slot, 4 * HEAD : 5 * HEAD, 64:] = key_b[:, tail]
            grads_send[slot, 5 * HEAD :, 64:] = value_b[:, tail]
    for k in range(1, 16):
        peer, device = at.group(k)
        send(grads_send.at[peer], grads_all.at[at.me], g_send.at[k], g_recv.at[k], device)
    grads_all[at.me] = grads_send[at.me]

    for k in range(1, 4):
        arrive(from_x.at[at.along_from("x", k)], s_send.at[8 + k], s_recv.at[8 + k])
    for z in range(4):
        to_z[z] = total_of(from_x, slice(z * HEAD, (z + 1) * HEAD)).astype(BF16)
    for k in range(1, 4):
        place, device = at.along("z", k)
        send(to_z.at[place], from_z.at[at.z], s_send.at[12 + k], s_recv.at[12 + k], device)
    from_z[at.z] = to_z[at.z]
    for k in range(1, 4):
        arrive(from_z.at[at.along_from("z", k)], s_send.at[12 + k], s_recv.at[12 + k])
    spread_bias((total_of(from_z) * TOKENS).astype(BF16), to_group)
    for k in range(1, 16):
        peer, device = at.group(k)
        send(to_group.at[peer], from_group.at[at.me], h_send.at[k], h_recv.at[k], device)
    from_group[at.me] = to_group[at.me]

    for k in range(1, 16):
        arrive(grads_all.at[at.group_from(k)], g_send.at[k], g_recv.at[k])
    tails = [back_piece(grads_all, 4), back_piece(grads_all, 5)]
    attended = jnp.concatenate([back_piece(grads_all, 0), tails[0][:64]], axis=0)
    grad_q = jnp.concatenate([back_piece(grads_all, 1), tails[1][:64]], axis=0)
    grad_k = jnp.concatenate([back_piece(grads_all, 2), tails[0][64:]], axis=0)
    grad_v = jnp.concatenate([back_piece(grads_all, 3), tails[1][64:]], axis=0)
    gamma = gamma_v[...]
    gate = gate_v[...]
    block_update = dot(attended, w_out[...])
    noised_f = noised[...].astype(F32)
    updated[...] = (noised_f + gate * block_update).astype(BF16)
    noised_norm, _ = norm_rows(noised_f)
    back = ((1,), (1,))
    grad_input = (
        dot(grad_q, w_query[...], back) + dot(grad_k, w_key[...], back) + dot(grad_v, w_value[...], back)
    )
    pre_gamma = (grad_input * noised_norm * (gamma * (1.0 - gamma))).astype(BF16)
    pre_gate = (cotangent[...].astype(F32) * block_update * (gate * (1.0 - gate))).astype(BF16)
    sums = dot(pre_gamma, w_gamma[...], back)
    sums = sums + dot(grad_input.astype(BF16), w_beta[...], back)
    sums = sums + dot(pre_gate, w_outgate[...], back)
    sums = sums.astype(BF16)
    for y in range(4):
        part[y] = sums[y * HEAD : (y + 1) * HEAD]

    sum_y[at.y] = part[at.y]
    for k in range(1, 4):
        place, device = at.along("y", k)
        send(part.at[place], sum_y.at[at.y], r_send.at[k], r_recv.at[k], device)
    for k in range(1, 16):
        arrive(from_group.at[at.group_from(k)], h_send.at[k], h_recv.at[k])
    grad_t = jnp.concatenate([from_group[h] for h in range(HEADS)], axis=0)
    grad_t = grad_t.astype(F32).T.astype(BF16)[:BLOCK]
    weight = pair_weight(w_pair_t)
    pair_back(grad_t, weight, pair, d_pair, range(0, 4))
    for k in range(1, 4):
        arrive(sum_y.at[at.along_from("y", k)], r_send.at[k], r_recv.at[k])
    sum_z[at.z] = total_of(sum_y).astype(BF16)
    for k in range(1, 4):
        rows = sum_z.at[at.z]
        send(rows, rows, r_send.at[4 + k], r_recv.at[4 + k], at.along("z", k)[1])
    pair_back(grad_t, weight, pair, d_pair, range(4, 9))
    for k in range(1, 4):
        arrive(sum_z.at[at.along_from("z", k)], r_send.at[4 + k], r_recv.at[4 + k])
    sum_x[at.x] = total_of(sum_z).astype(BF16)
    for k in range(1, 4):
        rows = sum_x.at[at.x]
        send(rows, rows, r_send.at[8 + k], r_recv.at[8 + k], at.along("x", k)[1])
    pair_back(grad_t, weight, pair, d_pair, range(9, ROWS))
    normed, inverse = norm_rows(single[pl.ds(at.y * HEAD, HEAD), :].astype(F32))
    for k in range(1, 4):
        arrive(sum_x.at[at.along_from("x", k)], r_send.at[8 + k], r_recv.at[8 + k])
    final = norm_back(total_of(sum_x), normed, inverse)
    own[...] = final
    d_single[at.y] = final
    for k in range(1, 4):
        send(own, d_single.at[at.y], r_send.at[12 + k], r_recv.at[12 + k], at.along("y", k)[1])
    for k in range(1, 4):
        arrive(d_single.at[at.along_from("y", k)], r_send.at[12 + k], r_recv.at[12 + k])
    for copy in out:
        copy.wait_send()


def on_device(
    single,
    pair,
    chains,
    noised,
    w_gamma,
    w_beta,
    w_outgate,
    w_query,
    w_key,
    w_value,
    w_out,
    w_pair,
    chain_gain,
    cotangent,
):
    def space(*shape):
        return pltpu.VMEM(shape, BF16)

    def wide_space(*shape):
        return pltpu.VMEM(shape, F32)

    def dma(count):
        return pltpu.SemaphoreType.DMA((count,))

    half_width = WIDTH // 2
    updated, d_single, d_pair = pl.pallas_call(
        block_kernel,
        out_shape=[
            jax.ShapeDtypeStruct((BLOCK, WIDTH), BF16),
            jax.ShapeDtypeStruct((4, HEAD, half_width), F32),
            jax.ShapeDtypeStruct(pair.shape, BF16),
        ],
        in_specs=[ANY] * 11 + [SMEM, VMEM, SMEM, VMEM],
        out_specs=[VMEM] * 3,
        scratch_shapes=[
            space(BLOCK, half_width),
            space(ROWS, BLOCK, 128),
            space(BLOCK, WIDTH),
            space(BLOCK, WIDTH),
        ]
        + [space(half_width, WIDTH)] * 3
        + [space(WIDTH, WIDTH)] * 4
        + [
            space(16, 16, 256),
            space(16, 16, 256),
            space(4, 4, HEAD, TOKENS),
            space(16, CHUNK, 128),
            space(16, CHUNK, 128),
            wide_space(BLOCK, WIDTH),
            wide_space(BLOCK, WIDTH),
            space(4, HEAD, TOKENS),
            space(4, HEAD, TOKENS),
            wide_space(4, HEAD, TOKENS),
            wide_space(4, HEAD, TOKENS),
            wide_space(BLOCK, TOKENS),
            space(4, BLOCK, TOKENS),
            space(4, BLOCK, TOKENS),
            space(4, HEAD, TOKENS),
            space(4, HEAD, TOKENS),
            space(16, 16, 256),
            space(16, 16, 256),
            space(16, CHUNK, 128),
            space(16, CHUNK, 128),
        ]
        + [space(4, HEAD, half_width)] * 4
        + [wide_space(HEAD, half_width)]
        + [dma(11)]
        + [dma(16)] * 12,
        compiler_params=pltpu.CompilerParams(
            vmem_limit_bytes=VMEM_BYTES, collective_id=0, has_side_effects=True
        ),
        name="block",
    )(
        single,
        pair,
        noised.reshape(BLOCK, WIDTH),
        cotangent.reshape(BLOCK, WIDTH),
        w_gamma,
        w_beta,
        w_outgate,
        w_query,
        w_key,
        w_value,
        w_out,
        chains,
        chains.reshape(1, TOKENS),
        chain_gain,
        w_pair.T,
    )
    return (
        updated.reshape(1, BLOCK, WIDTH),
        d_single.reshape(BLOCK, half_width),
        d_pair,
    )


def solution(mesh):
    rows = P("rows", "grp", None)
    grp = P("grp", None)
    in_specs = (grp, rows, P(), rows) + (P(),) * 9 + (rows,)
    return jax.shard_map(
        on_device, mesh=mesh, in_specs=in_specs, out_specs=(rows, grp, rows), check_vma=False
    )
```

time: 1300 us -> 99.7 us (0.08)
  waiting for transfers between devices: 773 us -> 0 us
  blocking collectives: 370 us -> 0 us
  Pallas kernels: 0 us -> 92.6 us
  matrix products: 65.6 us -> 0 us
  local copies, waits for them, and re-layouts: 56.3 us -> 5.54 us
  other arithmetic: 21.3 us -> 0 us
  between operations: 14.6 us -> 0.65 us
    psum x3 -> x0, blocking collectives: 370 us -> none  [the longest x1 346 us: on_device(): lax.psum((gamma_part, beta_part, gate_part), 'rows')]
    psum x1 -> x0, waiting for transfers between devices: 333 us -> none  [on_device(): lax.psum((gamma_part, beta_part, gate_part), 'rows')]
    reduce_scatter x1 -> x0, waiting for transfers between devices: 285 us -> none  [on_device(): lax.psum_scatter(bias_part, 'rows', scatter_dimension=1, tiled=True)]
    all_gather x3 -> x0, waiting for transfers between devices: 141 us -> none  [the longest x1 103 us: on_device(): bias_keys = lax.all_gather(bias_block, 'rows', axis=1, tiled=True)]
    pallas_call x0 -> x1, Pallas kernels: none -> 92.6 us  [on_device(): pl.pallas_call(block_kernel, out_shape=[jax.ShapeDtypeStruct((BLOCK, WIDT...]
    dot_general x22 -> x0, matrix products: 65.6 us -> none  [the longest x1 15.3 us: on_device(): jnp.einsum('sihe,sjhe->shij', grad_heads, value_heads, preferred_element_...]
    unnamed x74 -> x5, local copies, waits for them, and re-layouts: 30.3 us -> 4.27 us
    unnamed x9 -> x0, waiting for transfers between devices: 14 us -> none
  transfers between devices with their start and end apart: 7 -> 0, of which waited for: 6 -> 0; matrix products, arithmetic and copies ran while one was open for 5% -> 0% of each run, Pallas kernels for 0% -> 0%
where the time goes in v2:
time: 99.7 us; the launch traced here: 98.8 us
  Pallas kernels  92.6 us (93%)
  local copies, waits for them, and re-layouts  5.54 us (6%)
    pallas_call x1, Pallas kernels, on_device(): pl.pallas_call(block_kernel, out_shape=[jax.ShapeDtypeStruct((BLOCK, WIDT...  92.6 us
    unnamed x5, local copies, waits for them, and re-layouts  4.27 us

profile of v2, /device:TPU:2, one launch (start us, length us, event | category | flops | bytes accessed | tf_op | source)
XLA Modules:
  0.0 98.8 jit_solution(6978562177288868221)
XLA Ops:
  0.6 1.3 %reshape.23.chain_cols = s32[1,768]{1,0:T(1,128)} reshape(s32[768]{0:T(1024)} %chain_all.1) | data formatting | bytes 6144 | tf_op jit(solution)/shard_map/reshape | solution.py:541
  1.9 92.6 %block.1 = (bf16[192,768]{1,0:T(8,128)(2,1)}, f32[4,48,384]{2,1,0:T(8,128)}, bf16[12,192,128]{2,1,0:T(8,128)(2,1)}) custom-call(bf16[192,384]{1,0:T(8,128)(2,1)} %single_in.1, bf16[12,192,128]{2,1,0:T(8,128)(2,1)} %pair_in.1, bf16[192,768]{1,0:T(8,128)(2,1)} %bitcast.5, bf16[192,768]{1,0:T(8,128)(2,1)} %bitcast.6, bf16[384,768]{1,0:T(8,128)(2,1)} %w_gamma_in.1, ...), custom_call_target="tpu_custom_call" | custom-call | tf_op jit(solution)/shard_map/block/pallas_call | solution.py:481
  94.5 0.0 copy-start
  94.5 1.8 %copy.20 = bf16[1,192,768]{2,1,0:T(8,128)(2,1)} copy(bf16[1,192,768]{2,1,0:T(8,128)(2,1)} %bitcast.8) | data formatting | bytes 589824
  96.2 1.7 %copy.21 = f32[192,384]{1,0:T(8,128)} copy(f32[192,384]{1,0:T(8,128)} %bitcast.7) | data formatting | bytes 589824
  97.9 0.0 copy-done
  97.9 0.8 copy.22
Async XLA Ops:
  94.5 3.5 %copy-start = (bf16[12,192,128]{2,1,0:T(8,128)(2,1)S(1)}, bf16[12,192,128]{2,1,0:T(8,128)(2,1)}, u32[]{:S(2)}) copy-start(bf16[12,192,128]{2,1,0:T(8,128)(2,1)} %get-tuple-element.14) | copy-start | bytes 1769476

commit v3 on v2

v3 whole, which is shorter than its diff:
```python
import math

import jax
import jax.numpy as jnp
from jax import lax
from jax.experimental import pallas as pl
from jax.experimental.pallas import tpu as pltpu
from jax.sharding import PartitionSpec as P

EPSILON = 1e-05
LOG2E = math.log2(math.e)
F32 = jnp.float32
BF16 = jnp.bfloat16
MESH = pl.DeviceIdType.MESH
ANY = pl.BlockSpec(memory_space=pl.ANY)
VMEM = pl.BlockSpec(memory_space=pltpu.VMEM)
SMEM = pl.BlockSpec(memory_space=pltpu.SMEM)
VMEM_BYTES = 56 * 1024 * 1024

HEADS = 16
HEAD = 48
WIDTH = 768
TOKENS = 768
BLOCK = 192
ROWS = 12
CHUNK = 3 * HEAD


MIXED = (
    (1, 2), (3, 0), (2, 2), (1, 0), (3, 2), (2, 0), (0, 2), (0, 1),
    (1, 3), (3, 1), (2, 3), (1, 1), (3, 3), (2, 1), (0, 3),
)


def dot(left, right, contract=((1,), (0,))):
    return lax.dot_general(left, right, (contract, ((), ())), preferred_element_type=F32)


def norm_rows(values):
    center = values - jnp.mean(values, axis=-1, keepdims=True)
    inverse = lax.rsqrt(jnp.mean(center * center, axis=-1, keepdims=True) + EPSILON)
    return center * inverse, inverse


def norm_back(grad_in, normed, inverse):
    grad_mean = jnp.mean(grad_in, axis=-1, keepdims=True)
    cross_mean = jnp.mean(grad_in * normed, axis=-1, keepdims=True)
    return inverse * (grad_in - grad_mean - normed * cross_mean)


def iota(shape, dim):
    return lax.broadcasted_iota(jnp.int32, shape, dim)


class Place:
    def __init__(self):
        self.r = lax.axis_index("rows")
        self.b = lax.axis_index("grp")
        self.x = self.r // 16
        self.z = (self.r // 4) % 4
        self.y = self.r % 4
        self.me = self.y * 4 + self.b
        self.flip = 2 * (self.z % 2)
        self.head = self.y * 4 + (self.b + self.flip) % 4
        toward = 2 * (self.b // 2) - 1
        self.near = (self.z + 4 + toward) % 4
        self.far = (self.z + 4 - toward) % 4
        self.opposite = (self.z + 2) % 4

    def mate(self, dy, c):
        y = (self.y + dy) % 4
        b = (self.b + 2 * (c // 2)) % 4
        if c % 2:
            b = b + 1 - 2 * (b % 2)
        head = y * 4 + (b + self.flip) % 4
        return y * 4 + b, head, (self.r - self.y + y, b)

    def link(self, b):
        return 2 * ((self.b // 2 + b // 2) % 2) + (self.b + b) % 2

    def same_head(self, z):
        return (self.r + (z - self.z) * 4, (self.b + 2) % 4)

    def along(self, axis, k):
        if axis == "x":
            place = (self.x + k) % 4
            return place, (self.r + (place - self.x) * 16, self.b)
        if axis == "z":
            place = (self.z + k) % 4
            return place, (self.r + (place - self.z) * 4, self.b)
        place = (self.y + k) % 4
        return place, (self.r + (place - self.y), self.b)

    def along_from(self, axis, k):
        return ({"x": self.x, "z": self.z, "y": self.y}[axis] + 4 - k) % 4


def remote(source, target, send, recv, device):
    return pltpu.make_async_remote_copy(
        src_ref=source,
        dst_ref=target,
        send_sem=send,
        recv_sem=recv,
        device_id=device,
        device_id_type=MESH,
    )


def total_of(ref, rows=slice(None)):
    value = ref[0, rows, :].astype(F32)
    for n in range(1, 4):
        value = value + ref[n, rows, :].astype(F32)
    return value


def pair_bias(pair, chain_cols, chain_all, chain_gain, w_pair_t, at, bias_send):
    cols = chain_cols[...]
    mine = cols[:, :BLOCK]
    for b in range(1, 4):
        mine = jnp.where(at.b == b, cols[:, b * BLOCK : (b + 1) * BLOCK], mine)
    head = iota((HEADS, 1), 0)
    gain = jnp.zeros((HEADS, 1), F32)
    for h in range(HEADS):
        gain = jnp.where(head == h, chain_gain[h], gain)
    strips = []
    for i in range(ROWS):
        normed, _ = norm_rows(pair[i].astype(F32))
        projected = dot(w_pair_t[...], normed.astype(BF16), ((1,), (1,)))
        same = (mine == chain_all[at.r * ROWS + i]).astype(F32)
        strips.append((projected + gain * same).astype(BF16))
    strips = jnp.concatenate(strips, axis=0)
    shape = (HEADS * 16, HEADS * ROWS)
    to, source = iota(shape, 0), iota(shape, 1)
    order = ((to // 16 == source % 16) & (to % 16 == source // 16)).astype(BF16)
    spread = dot(order, strips).astype(BF16)
    for h in range(HEADS):
        rows = spread[h * 16 : (h + 1) * 16]
        bias_send[h, :, :128] = rows[:, :128]
        bias_send[h, :, 128:] = jnp.concatenate([rows[:, 128:], jnp.zeros((16, 64), BF16)], axis=1)


def make_acts(noised, cotangent, gamma, beta, gate, w_query, w_key, w_value, w_out, acts_send):
    noised_norm, _ = norm_rows(noised[...].astype(F32))
    x_b = (noised_norm * gamma + beta).astype(BF16)
    grad_update = (cotangent[...].astype(F32) * gate).astype(BF16)
    arrays = (
        (dot(x_b, w_key[...]), dot(x_b, w_value[...])),
        (dot(x_b, w_query[...]), dot(grad_update, w_out[...], ((1,), (1,)))),
    )
    for part, (first, second) in enumerate(arrays):
        tail = jnp.concatenate([first[128:], second[128:]], axis=0)
        for n, piece in enumerate((first[:128], second[:128], tail)):
            piece = piece.T.astype(BF16)
            for h in range(HEADS):
                acts_send[h, part, n * HEAD : (n + 1) * HEAD, :] = piece[h * HEAD : (h + 1) * HEAD]


def assemble_bias(held):
    strips = []
    for y in range(4):
        parts = [held[y * 4 + b] for b in range(4)]
        tails = [p[:, 128:BLOCK] for p in parts]
        strips.append(jnp.concatenate([p[:, :128] for p in parts] + tails, axis=1))
    strips = jnp.concatenate(strips, axis=0)
    to, source = iota((HEAD, 64), 0), iota((HEAD, 64), 1)
    pick = ((source // 16 == to // ROWS) & (source % 16 == to % ROWS)).astype(BF16)
    return dot(pick, strips).astype(BF16)


def spread_bias(total, to_group):
    to, source = iota((64, HEAD), 0), iota((64, HEAD), 1)
    pick = ((to // 16 == source // ROWS) & (to % 16 == source % ROWS)).astype(BF16)
    spread = dot(pick, total).astype(BF16)
    for y in range(4):
        rows = spread[y * 16 : (y + 1) * 16]
        for b in range(4):
            tail = rows[:, 512 + b * 64 : 512 + (b + 1) * 64]
            to_group[y * 4 + b, :, :128] = rows[:, b * 128 : (b + 1) * 128]
            to_group[y * 4 + b, :, 128:] = jnp.concatenate([tail, jnp.zeros_like(tail)], axis=1)


def half(n):
    return slice(n * 64, n * 64 + 64)


def wide(acts, first, n):
    parts = [acts[first + b, 0, n * HEAD : (n + 1) * HEAD, :] for b in range(4)]
    parts += [acts[first + b, 0, 2 * HEAD :, half(n)] for b in range(4)]
    return jnp.concatenate(parts, axis=1)


def block(acts, place, n):
    return jnp.concatenate(
        [acts[place, 1, n * HEAD : (n + 1) * HEAD, :], acts[place, 1, 2 * HEAD :, half(n)]], axis=1
    )


def attend(query_t, grad_t, key_t, value_t, bias):
    scale = 1.0 / math.sqrt(HEAD)
    query = query_t.astype(F32).T.astype(BF16)
    grad = grad_t.astype(F32).T.astype(BF16)
    scores = dot(query, key_t) * (scale * LOG2E) + bias
    weight = jnp.exp2(scores)
    prob = weight * (1.0 / jnp.sum(weight, axis=-1, keepdims=True))
    grad_prob = dot(grad, value_t)
    scaled = prob * grad_prob
    grad_score = scaled - prob * jnp.sum(scaled, axis=-1, keepdims=True)
    return prob.astype(BF16), grad_score.astype(BF16), grad_score


def back_pieces(grads, part):
    def piece(n):
        rows = [grads[h, part, n * HEAD : (n + 1) * HEAD, :] for h in range(HEADS)]
        return jnp.concatenate(rows, axis=0).astype(F32).T.astype(BF16)

    tail = piece(2)
    return [jnp.concatenate([piece(n), tail[n * 64 : n * 64 + 64]], axis=0) for n in (0, 1)]


def pair_weight(w_pair_t):
    shape = (HEADS * 16, HEADS)
    pick = (iota(shape, 0) // 16 == iota(shape, 1)).astype(BF16)
    return dot(pick, w_pair_t[...]).astype(BF16)


def pair_back(grad_t, weight, pair, result, rows):
    row = iota(weight.shape, 0) % 16
    for i in rows:
        grad = dot(grad_t, jnp.where(row == i, weight, jnp.zeros_like(weight)))
        normed, inverse = norm_rows(pair[i].astype(F32))
        result[i] = norm_back(grad, normed, inverse).astype(BF16)


def block_kernel(
    single_in, pair_in, noised_in, cotangent_in,
    w_gamma_in, w_beta_in, w_outgate_in, w_query_in, w_key_in, w_value_in, w_out_in,
    chain_in, cols_in, gain_in, w_pair_in,
    updated_out, d_single, d_pair_out,
    single, pair, noised, cotangent, w_gamma, w_beta, w_outgate, w_query, w_key, w_value, w_out,
    bias_send, held, bias_all, acts_send, acts_all, gamma_v, gate_v, bias_f,
    key_t, value_t, grad_key, grad_value,
    to_x, from_x, to_z, from_z, to_group, from_group, grads_send, grads_all,
    part, sum_y, sum_z, sum_x, updated, d_pair, sums_v, inner_v, chain_all, chain_cols, chain_gain, w_pair_t,
    load, a_send, a_recv, q_send, q_recv, b_send, b_recv, g_send, g_recv, o_send, o_recv, h_send, h_recv,
    x_send, x_recv, u_send, u_recv, z_send, z_recv, r_send, r_recv,
):
    at = Place()
    barrier = pltpu.get_barrier_semaphore()
    mates = [(dy, c) for dy in (1, 2, 3, 0) for c in (2, 3, 0, 1) if (dy, c) != (0, 0)]
    peers = (
        [at.along("z", k)[1] for k in (2, 1, 3)]
        + [at.same_head(at.far), at.same_head(at.near)]
        + [at.along("x", k)[1] for k in (2, 1, 3)]
        + [at.mate(dy, c)[2] for dy, c in mates]
    )
    for device in peers:
        pl.semaphore_signal(barrier, inc=1, device_id=device, device_id_type=MESH)
    loads = {}
    for n, (name, source, target) in enumerate(
        (
            ("chain", chain_in, chain_all),
            ("gain", gain_in, chain_gain),
            ("cols", cols_in, chain_cols),
            ("map", w_pair_in, w_pair_t),
            ("pair", pair_in, pair),
            ("single", single_in, single),
            ("gamma", w_gamma_in, w_gamma),
            ("beta", w_beta_in, w_beta),
            ("gate", w_outgate_in, w_outgate),
            ("noised", noised_in, noised),
            ("query", w_query_in, w_query),
            ("key", w_key_in, w_key),
            ("value", w_value_in, w_value),
            ("cot", cotangent_in, cotangent),
            ("out", w_out_in, w_out),
        )
    ):
        loads[name] = pltpu.make_async_copy(source, target, load.at[n])
        loads[name].start()
    out = []

    def send(source, target, ssem, rsem, device):
        copy = remote(source, target, ssem, rsem, device)
        copy.start()
        out.append(copy)

    def arrive(buffer, ssem, rsem):
        remote(buffer, buffer, ssem, rsem, at.along("x", 1)[1]).wait_recv()

    def send_acts(part, dy, c):
        _, head, device = at.mate(dy, c)
        n = dy * 4 + c
        ssem, rsem = ((a_send, a_recv), (q_send, q_recv))[part]
        send(acts_send.at[head, part], acts_all.at[at.me, part], ssem.at[n], rsem.at[n], device)

    def send_all_acts(part):
        for dy, c in MIXED:
            send_acts(part, dy, c)

    for name in ("chain", "gain", "cols", "map", "pair"):
        loads[name].wait()
    pair_bias(pair, chain_cols, chain_all, chain_gain, w_pair_t, at, bias_send)
    pl.semaphore_wait(barrier, len(peers))
    for dy, c in mates:
        _, head, device = at.mate(dy, c)
        n = dy * 4 + c
        send(bias_send.at[head], held.at[at.me], b_send.at[n], b_recv.at[n], device)
    held[at.me] = bias_send[at.head]
    for name in ("single", "gamma", "beta", "gate", "noised", "query", "key", "value", "cot", "out"):
        loads[name].wait()
    single_norm, _ = norm_rows(single[...].astype(F32))
    single_b = single_norm.astype(BF16)
    gamma = jax.nn.sigmoid(dot(single_b, w_gamma[...]))
    beta = dot(single_b, w_beta[...])
    gate = jax.nn.sigmoid(dot(single_b, w_outgate[...]))
    gamma_v[...] = gamma
    gate_v[...] = gate
    make_acts(noised, cotangent, gamma, beta, gate, w_query, w_key, w_value, w_out, acts_send)
    send_all_acts(0)
    acts_all[at.me] = acts_send[at.head]
    for dy, c in mates:
        n = dy * 4 + c
        arrive(held.at[at.mate(4 - dy, c)[0]], b_send.at[n], b_recv.at[n])
    bias_all[at.x, at.z] = assemble_bias(held)
    order = (at.z, at.near, at.far, at.opposite)
    rows = bias_all.at[at.x, at.z]
    send(rows, rows, z_send.at[2], z_recv.at[2], at.same_head(at.far))
    send(rows, rows, z_send.at[1], z_recv.at[1], at.same_head(at.near))
    for kz in range(4):
        rows = bias_all.at[at.x, order[kz]]
        if kz:
            arrive(rows, z_send.at[kz], z_recv.at[kz])
        if kz == 2:
            send(rows, rows, z_send.at[3], z_recv.at[3], at.same_head(at.near))
        for k in (2, 1, 3):
            n = k * 4 + kz
            send(rows, rows, x_send.at[n], x_recv.at[n], at.along("x", k)[1])
        if kz == 0:
            send_all_acts(1)
    samples = [(at.y + 4 - dy) % 4 for dy in (1, 2, 3, 0)]
    for s, dy in enumerate((1, 2, 3, 0)):
        for c in range(4):
            if dy or c:
                n = dy * 4 + c
                arrive(acts_all.at[at.mate(4 - dy, c)[0], 0], a_send.at[n], a_recv.at[n])
        key_t[s] = wide(acts_all, samples[s] * 4, 0)
        value_t[s] = wide(acts_all, samples[s] * 4, 1)
        grad_key[s] = jnp.zeros((HEAD, TOKENS), F32)
        grad_value[s] = jnp.zeros((HEAD, TOKENS), F32)

    scale = 1.0 / math.sqrt(HEAD)

    def step_body(step, carry):
        k = step + step // 2 - 2 * (step // 3)
        place, device = at.along("x", k)
        c = at.link(place)

        @pl.when(step > 0)
        def _():
            for kz in range(4):
                n = (4 - k) * 4 + kz
                arrive(bias_all.at[place, order[kz]], x_send.at[n], x_recv.at[n])

        @pl.when(c > 0)
        def _():
            arrive(acts_all.at[at.y * 4 + place, 1], q_send.at[c], q_recv.at[c])

        for s, dy in enumerate((1, 2, 3)):
            n = dy * 4 + c
            arrive(acts_all.at[samples[s] * 4 + place, 1], q_send.at[n], q_recv.at[n])
        for z in range(4):
            bias_f[z * HEAD : (z + 1) * HEAD, :] = bias_all[place, z].astype(F32) * LOG2E

        def weigh(s):
            slot = samples[s] * 4 + place
            query_t = block(acts_all, slot, 0)
            grad_t = block(acts_all, slot, 1)
            return (query_t, grad_t) + attend(query_t, grad_t, key_t[s], value_t[s], bias_f[...])

        ahead = weigh(0)
        total = ahead[4]
        for s, dy in enumerate((1, 2, 3, 0)):
            query_t, grad_t, prob_b, score_b, _ = ahead
            if s < 3:
                ahead = weigh(s + 1)
                total = total + ahead[4]
            slot = samples[s] * 4 + place
            attended = dot(value_t[s], prob_b, ((1,), (1,))).astype(BF16)
            grad_query = (dot(key_t[s], score_b, ((1,), (1,))) * scale).astype(BF16)
            grad_value[s] = grad_value[s] + dot(grad_t, prob_b)
            grad_key[s] = grad_key[s] + dot(query_t, score_b)
            grads_send[slot, 1, :HEAD, :] = attended[:, :128]
            grads_send[slot, 1, HEAD : 2 * HEAD, :] = grad_query[:, :128]
            grads_send[slot, 1, 2 * HEAD :, :64] = attended[:, 128:]
            grads_send[slot, 1, 2 * HEAD :, 64:] = grad_query[:, 128:]
        for z in range(4):
            to_x[k, z] = total[z * HEAD : (z + 1) * HEAD].astype(BF16)

        @pl.when(step > 0)
        def _():
            for kz in (3, 2, 1, 0):
                z = order[kz]
                n = k * 4 + kz
                remote(to_x.at[k, z], from_x.at[at.x, z], u_send.at[n], u_recv.at[n], device).start()

        for s, dy in enumerate((1, 2, 3, 0)):
            slot = samples[s] * 4 + place
            n = (4 - dy) % 4 * 4 + c
            copy = remote(
                grads_send.at[slot, 1],
                grads_all.at[at.head, 1],
                o_send.at[n],
                o_recv.at[n],
                (at.r - at.y + samples[s], place),
            )
            if dy:
                copy.start()
            else:
                pl.when(c > 0)(copy.start)
        return carry

    lax.fori_loop(0, 4, step_body, 0)
    for s, dy in enumerate((1, 2, 3, 0)):
        key_b = (grad_key[s] * scale).astype(BF16)
        value_b = grad_value[s].astype(BF16)
        for b in range(4):
            slot = samples[s] * 4 + b
            lanes = slice(b * 128, (b + 1) * 128)
            tail = slice(512 + b * 64, 512 + (b + 1) * 64)
            grads_send[slot, 0, :HEAD, :] = key_b[:, lanes]
            grads_send[slot, 0, HEAD : 2 * HEAD, :] = value_b[:, lanes]
            grads_send[slot, 0, 2 * HEAD :, :64] = key_b[:, tail]
            grads_send[slot, 0, 2 * HEAD :, 64:] = value_b[:, tail]
        for c in (2, 0, 3, 1):
            if dy or c:
                slot, _, device = at.mate(4 - dy, c)
                n = (4 - dy) % 4 * 4 + c
                send(
                    grads_send.at[slot, 0], grads_all.at[at.head, 0], g_send.at[n], g_recv.at[n], device
                )
    for dy, c in mates:
        slot, _, device = at.mate(dy, c)
        n = dy * 4 + c
        out.append(
            remote(grads_send.at[slot, 1], grads_all.at[at.head, 1], o_send.at[n], o_recv.at[n], device)
        )
    for k in range(1, 4):
        for kz in range(4):
            z = order[kz]
            n = k * 4 + kz
            device = at.along("x", k)[1]
            out.append(remote(to_x.at[k, z], from_x.at[at.x, z], u_send.at[n], u_recv.at[n], device))
    grads_all[at.head] = grads_send[at.me]
    from_x[at.x] = to_x[0]

    for dy, c in mates:
        n = dy * 4 + c
        arrive(grads_all.at[at.mate(4 - dy, c)[1], 1], o_send.at[n], o_recv.at[n])
    attended, grad_q = back_pieces(grads_all, 1)
    gamma = gamma_v[...]
    gate = gate_v[...]
    block_update = dot(attended, w_out[...])
    noised_f = noised[...].astype(F32)
    updated[...] = (noised_f + gate * block_update).astype(BF16)
    noised_norm, _ = norm_rows(noised_f)
    back = ((1,), (1,))
    pre_gate = (cotangent[...].astype(F32) * block_update * (gate * (1.0 - gate))).astype(BF16)
    sums_v[...] = dot(pre_gate, w_outgate[...], back)
    inner_v[...] = dot(grad_q, w_query[...], back)
    gamma_v[...] = noised_norm * (gamma * (1.0 - gamma))
    save = pltpu.make_async_copy(updated, updated_out, load.at[0])
    save.start()

    def rows_for(kz):
        z = order[kz]
        for k in range(1, 4):
            n = k * 4 + kz
            arrive(from_x.at[at.along_from("x", k), z], u_send.at[n], u_recv.at[n])
        rows = from_x[0, z].astype(F32)
        for x in range(1, 4):
            rows = rows + from_x[x, z].astype(F32)
        return rows

    to_z[3] = rows_for(3).astype(BF16)
    send(to_z.at[3], from_z.at[3], z_send.at[7], z_recv.at[7], at.same_head(at.near))
    to_z[1] = rows_for(1).astype(BF16)
    send(to_z.at[1], from_z.at[1], z_send.at[5], z_recv.at[5], at.same_head(at.near))
    for dy, c in mates:
        n = dy * 4 + c
        arrive(grads_all.at[at.mate(4 - dy, c)[1], 0], g_send.at[n], g_recv.at[n])
    grad_k, grad_v = back_pieces(grads_all, 0)
    grad_input = inner_v[...] + dot(grad_k, w_key[...], back) + dot(grad_v, w_value[...], back)
    pre_gamma = (grad_input * gamma_v[...]).astype(BF16)
    sums = sums_v[...] + dot(pre_gamma, w_gamma[...], back)
    sums = sums + dot(grad_input.astype(BF16), w_beta[...], back)
    sums = sums.astype(BF16)
    for y in range(4):
        part[y] = sums[y * HEAD : (y + 1) * HEAD]
    for k in (2, 1, 3):
        place, device = at.along("y", k)
        send(part.at[place], sum_y.at[at.y], r_send.at[k], r_recv.at[k], device)
    sum_y[at.y] = part[at.y]

    to_far = rows_for(2)
    arrive(from_z.at[3], z_send.at[7], z_recv.at[7])
    to_z[2] = (to_far + from_z[3].astype(F32)).astype(BF16)
    send(to_z.at[2], from_z.at[2], z_send.at[6], z_recv.at[6], at.same_head(at.far))
    for k in range(1, 4):
        arrive(sum_y.at[at.along_from("y", k)], r_send.at[k], r_recv.at[k])
    sum_z[at.z] = total_of(sum_y).astype(BF16)
    for k in (2, 1, 3):
        rows = sum_z.at[at.z]
        send(rows, rows, r_send.at[4 + k], r_recv.at[4 + k], at.along("z", k)[1])
    own_rows = rows_for(0)
    weight = pair_weight(w_pair_t)
    normed, inverse = norm_rows(single[pl.ds(at.y * HEAD, HEAD), :].astype(F32))
    for kz in (1, 2):
        arrive(from_z.at[kz], z_send.at[4 + kz], z_recv.at[4 + kz])
    own_rows = own_rows + from_z[1].astype(F32) + from_z[2].astype(F32)
    spread_bias((own_rows * TOKENS).astype(BF16), to_group)
    for dy, c in mates:
        slot, _, device = at.mate(dy, c)
        n = dy * 4 + c
        send(to_group.at[slot], from_group.at[at.head], h_send.at[n], h_recv.at[n], device)
    from_group[at.head] = to_group[at.me]
    for k in range(1, 4):
        arrive(sum_z.at[at.along_from("z", k)], r_send.at[4 + k], r_recv.at[4 + k])
    sum_x[at.x] = total_of(sum_z).astype(BF16)
    for k in (2, 1, 3):
        rows = sum_x.at[at.x]
        send(rows, rows, r_send.at[8 + k], r_recv.at[8 + k], at.along("x", k)[1])
    for dy, c in mates:
        n = dy * 4 + c
        arrive(from_group.at[at.mate(4 - dy, c)[1]], h_send.at[n], h_recv.at[n])
    grad_t = jnp.concatenate([from_group[h] for h in range(HEADS)], axis=0)
    grad_t = grad_t.astype(F32).T.astype(BF16)[:BLOCK]
    pair_back(grad_t, weight, pair, d_pair, range(0, 6))
    for k in range(1, 4):
        arrive(sum_x.at[at.along_from("x", k)], r_send.at[8 + k], r_recv.at[8 + k])
    d_single[at.y] = norm_back(total_of(sum_x), normed, inverse).astype(BF16)
    for k in (2, 1, 3):
        rows = d_single.at[at.y]
        send(rows, rows, r_send.at[12 + k], r_recv.at[12 + k], at.along("y", k)[1])
    pair_back(grad_t, weight, pair, d_pair, range(6, ROWS))
    keep = pltpu.make_async_copy(d_pair, d_pair_out, load.at[1])
    keep.start()
    save.wait()
    keep.wait()
    for k in range(1, 4):
        arrive(d_single.at[at.along_from("y", k)], r_send.at[12 + k], r_recv.at[12 + k])
    for copy in out:
        copy.wait_send()


def finish_kernel(updated_in, d_single_in, d_pair_in, updated, d_single, d_pair):
    updated[...] = updated_in[...]
    d_single[...] = d_single_in[...].astype(F32)
    d_pair[...] = d_pair_in[...]


def on_device(
    single,
    pair,
    chains,
    noised,
    w_gamma,
    w_beta,
    w_outgate,
    w_query,
    w_key,
    w_value,
    w_out,
    w_pair,
    chain_gain,
    cotangent,
):
    def space(*shape):
        return pltpu.VMEM(shape, BF16)

    def wide_space(*shape):
        return pltpu.VMEM(shape, F32)

    def dma(count):
        return pltpu.SemaphoreType.DMA((count,))

    half_width = WIDTH // 2
    results = pl.pallas_call(
        block_kernel,
        out_shape=[
            jax.ShapeDtypeStruct((BLOCK, WIDTH), BF16),
            jax.ShapeDtypeStruct((4, HEAD, half_width), BF16),
            jax.ShapeDtypeStruct(pair.shape, BF16),
        ],
        in_specs=[ANY] * 15,
        out_specs=[ANY, VMEM, ANY],
        scratch_shapes=[
            space(BLOCK, half_width),
            space(ROWS, BLOCK, 128),
            space(BLOCK, WIDTH),
            space(BLOCK, WIDTH),
        ]
        + [space(half_width, WIDTH)] * 3
        + [space(WIDTH, WIDTH)] * 4
        + [
            space(16, 16, 256),
            space(16, 16, 256),
            space(4, 4, HEAD, TOKENS),
            space(16, 2, CHUNK, 128),
            space(16, 2, CHUNK, 128),
            wide_space(BLOCK, WIDTH),
            wide_space(BLOCK, WIDTH),
            wide_space(BLOCK, TOKENS),
            space(4, HEAD, TOKENS),
            space(4, HEAD, TOKENS),
            wide_space(4, HEAD, TOKENS),
            wide_space(4, HEAD, TOKENS),
            space(4, 4, HEAD, TOKENS),
            space(4, 4, HEAD, TOKENS),
            space(4, HEAD, TOKENS),
            space(4, HEAD, TOKENS),
            space(16, 16, 256),
            space(16, 16, 256),
            space(16, 2, CHUNK, 128),
            space(16, 2, CHUNK, 128),
        ]
        + [space(4, HEAD, half_width)] * 4
        + [space(BLOCK, WIDTH), space(ROWS, BLOCK, 128)]
        + [wide_space(BLOCK, half_width), wide_space(BLOCK, WIDTH)]
        + [
            pltpu.SMEM((TOKENS,), jnp.int32),
            pltpu.VMEM((1, TOKENS), jnp.int32),
            pltpu.SMEM((HEADS,), F32),
            space(HEADS, 128),
        ]
        + [dma(15)]
        + [dma(16)] * 20,
        compiler_params=pltpu.CompilerParams(
            vmem_limit_bytes=VMEM_BYTES, collective_id=0, has_side_effects=True
        ),
        name="block",
    )(
        single,
        pair,
        noised.reshape(BLOCK, WIDTH),
        cotangent.reshape(BLOCK, WIDTH),
        w_gamma,
        w_beta,
        w_outgate,
        w_query,
        w_key,
        w_value,
        w_out,
        chains,
        chains.reshape(1, TOKENS),
        chain_gain,
        w_pair.T,
    )
    updated, d_single, d_pair = pl.pallas_call(
        finish_kernel,
        out_shape=[
            jax.ShapeDtypeStruct((BLOCK, WIDTH), BF16),
            jax.ShapeDtypeStruct((BLOCK, half_width), F32),
            jax.ShapeDtypeStruct(pair.shape, BF16),
        ],
        in_specs=[VMEM] * 3,
        out_specs=[VMEM] * 3,
        name="finish",
    )(results[0], results[1].reshape(BLOCK, half_width), results[2])
    return updated.reshape(1, BLOCK, WIDTH), d_single, d_pair


def solution(mesh):
    rows = P("rows", "grp", None)
    grp = P("grp", None)
    in_specs = (grp, rows, P(), rows) + (P(),) * 9 + (rows,)
    return jax.shard_map(
        on_device, mesh=mesh, in_specs=in_specs, out_specs=(rows, grp, rows), check_vma=False
    )
```

time: 99.7 us -> 77.8 us (0.78)
  Pallas kernels: 92.6 us -> 75.3 us
  local copies, waits for them, and re-layouts: 5.54 us -> 1.27 us
    pallas_call x1, Pallas kernels: 92.6 us -> 73 us  [on_device(): pl.pallas_call(block_kernel, out_shape=[jax.ShapeDtypeStruct((BLOCK, WIDT...]
    unnamed x5 -> x0, local copies, waits for them, and re-layouts: 4.27 us -> none
    pallas_call x0 -> x1, Pallas kernels: none -> 2.27 us  [on_device(): pl.pallas_call(finish_kernel, out_shape=[jax.ShapeDtypeStruct((BLOCK, WID...]
where the time goes in v3:
time: 77.8 us; the launch traced here: 77.2 us
  Pallas kernels  75.3 us (97%)
  local copies, waits for them, and re-layouts  1.27 us (2%)
    pallas_call x1, Pallas kernels, on_device(): pl.pallas_call(block_kernel, out_shape=[jax.ShapeDtypeStruct((BLOCK, WIDT...  73 us
    pallas_call x1, Pallas kernels, on_device(): pl.pallas_call(finish_kernel, out_shape=[jax.ShapeDtypeStruct((BLOCK, WID...  2.27 us

profile of v3, /device:TPU:2, one launch (start us, length us, event | category | flops | bytes accessed | tf_op | source)
XLA Modules:
  0.0 77.2 jit_solution(7599239385365934918)
XLA Ops:
  0.6 1.3 %reshape.23.cols_in = s32[1,768]{1,0:T(1,128)} reshape(s32[768]{0:T(1024)} %chain_in.1) | data formatting | bytes 6144 | tf_op jit(solution)/shard_map/reshape | solution.py:654
  1.9 73.0 %block.1 = (bf16[192,768]{1,0:T(8,128)(2,1)}, bf16[4,48,384]{2,1,0:T(8,128)(2,1)}, bf16[12,192,128]{2,1,0:T(8,128)(2,1)}) custom-call(bf16[192,384]{1,0:T(8,128)(2,1)} %single_in.1, bf16[12,192,128]{2,1,0:T(8,128)(2,1)} %pair_in.1, bf16[192,768]{1,0:T(8,128)(2,1)} %bitcast.5, bf16[192,768]{1,0:T(8,128)(2,1)} %bitcast.6, bf16[384,768]{1,0:T(8,128)(2,1)} %w_gamma_in.1, ...), custom_call_target="tpu_custom_call" | custom-call | tf_op jit(solution)/shard_map/block/pallas_call | solution.py:587
  74.9 2.3 %finish.1 = (bf16[192,768]{1,0:T(8,128)(2,1)}, f32[192,384]{1,0:T(8,128)}, bf16[12,192,128]{2,1,0:T(8,128)(2,1)}) custom-call(bf16[192,768]{1,0:T(8,128)(2,1)} %get-tuple-element.9.updated_in, bf16[192,384]{1,0:T(8,128)(2,1)} %bitcast.7, bf16[12,192,128]{2,1,0:T(8,128)(2,1)} %get-tuple-element.11.d_pair_in), custom_call_target="tpu_custom_call" | custom-call | tf_op jit(solution)/shard_map/finish/pallas_call | solution.py:658

commit v4 on v3

--- a/solution.py
+++ b/solution.py
@@ -59,6 +59,7 @@
         self.x = self.r // 16
         self.z = (self.r // 4) % 4
         self.y = self.r % 4
+        self.spot = self.x * 4 + self.y
         self.me = self.y * 4 + self.b
         self.flip = 2 * (self.z % 2)
         self.head = self.y * 4 + (self.b + self.flip) % 4
@@ -80,6 +81,10 @@
 
     def same_head(self, z):
         return (self.r + (z - self.z) * 4, (self.b + 2) % 4)
+
+    def plane(self, dx, dy):
+        x, y = (self.x + dx) % 4, (self.y + dy) % 4
+        return x * 4 + y, (self.r + (x - self.x) * 16 + (y - self.y), self.b)
 
     def along(self, axis, k):
         if axis == "x":
@@ -208,6 +213,12 @@
     return prob.astype(BF16), grad_score.astype(BF16), grad_score
 
 
+def thin_rows(spread):
+    shape = (16 * 16, BLOCK) if spread else (BLOCK, 16 * 16)
+    thin, full = iota(shape, 0 if spread else 1), iota(shape, 1 if spread else 0)
+    return ((thin // 16 == full // ROWS) & (thin % 16 == full % ROWS)).astype(BF16)
+
+
 def back_pieces(grads, part):
     def piece(n):
         rows = [grads[h, part, n * HEAD : (n + 1) * HEAD, :] for h in range(HEADS)]
@@ -235,26 +246,25 @@
     single_in, pair_in, noised_in, cotangent_in,
     w_gamma_in, w_beta_in, w_outgate_in, w_query_in, w_key_in, w_value_in, w_out_in,
     chain_in, cols_in, gain_in, w_pair_in,
-    updated_out, d_single, d_pair_out,
+    updated_out, plane_out, d_pair_out,
     single, pair, noised, cotangent, w_gamma, w_beta, w_outgate, w_query, w_key, w_value, w_out,
     bias_send, held, bias_all, acts_send, acts_all, gamma_v, gate_v, bias_f,
     key_t, value_t, grad_key, grad_value,
     to_x, from_x, to_z, from_z, to_group, from_group, grads_send, grads_all,
-    part, sum_y, sum_z, sum_x, updated, d_pair, sums_v, inner_v, chain_all, chain_cols, chain_gain, w_pair_t,
-    load, a_send, a_recv, q_send, q_recv, b_send, b_recv, g_send, g_recv, o_send, o_recv, h_send, h_recv,
-    x_send, x_recv, u_send, u_recv, z_send, z_recv, r_send, r_recv,
+    part, plane_in, sum_z, own, updated, d_pair, sums_v, inner_v, chain_all, chain_cols, chain_gain, w_pair_t,
+    load, sent, got, q_recv, x_recv, u_recv, z_recv,
 ):
     at = Place()
     barrier = pltpu.get_barrier_semaphore()
+    others = [(dx, dy) for dx in (2, 1, 3, 0) for dy in (2, 1, 3, 0) if dx or dy]
     mates = [(dy, c) for dy in (1, 2, 3, 0) for c in (2, 3, 0, 1) if (dy, c) != (0, 0)]
     peers = (
         [at.along("z", k)[1] for k in (2, 1, 3)]
         + [at.same_head(at.far), at.same_head(at.near)]
         + [at.along("x", k)[1] for k in (2, 1, 3)]
         + [at.mate(dy, c)[2] for dy, c in mates]
+        + [at.plane(dx, dy)[1] for dx, dy in others if dx and dy]
     )
-    for device in peers:
-        pl.semaphore_signal(barrier, inc=1, device_id=device, device_id_type=MESH)
     loads = {}
     for n, (name, source, target) in enumerate(
         (
@@ -277,25 +287,24 @@
     ):
         loads[name] = pltpu.make_async_copy(source, target, load.at[n])
         loads[name].start()
-    out = []
+        if name == "pair":
+            for device in peers:
+                pl.semaphore_signal(barrier, inc=1, device_id=device, device_id_type=MESH)
 
     def send(source, target, ssem, rsem, device):
-        copy = remote(source, target, ssem, rsem, device)
-        copy.start()
-        out.append(copy)
-
-    def arrive(buffer, ssem, rsem):
-        remote(buffer, buffer, ssem, rsem, at.along("x", 1)[1]).wait_recv()
-
-    def send_acts(part, dy, c):
-        _, head, device = at.mate(dy, c)
-        n = dy * 4 + c
-        ssem, rsem = ((a_send, a_recv), (q_send, q_recv))[part]
-        send(acts_send.at[head, part], acts_all.at[at.me, part], ssem.at[n], rsem.at[n], device)
-
-    def send_all_acts(part):
-        for dy, c in MIXED:
-            send_acts(part, dy, c)
+        remote(source, target, ssem, rsem, device).start()
+
+    def arrive(buffer, rsem):
+        remote(buffer, buffer, sent.at[0], rsem, at.along("x", 1)[1]).wait_recv()
+
+    def left(buffer, ssem):
+        remote(buffer, buffer, ssem, got.at[0], at.along("x", 1)[1]).wait_send()
+
+    bias_sent, kv_sent, q_sent, z_sent, x_sent, rows_sent, grads_sent = [sent.at[n] for n in range(7)]
+    u_sent, near_sent, group_sent, plane_sent, sum_sent, out_sent = [sent.at[n] for n in range(7, 13)]
+    bias_got, kv_got, rows_got, grads_got, group_got, plane_got, sum_got, out_got = [
+        got.at[n] for n in range(8)
+    ]
 
     for name in ("chain", "gain", "cols", "map", "pair"):
         loads[name].wait()
@@ -303,8 +312,7 @@
     pl.semaphore_wait(barrier, len(peers))
     for dy, c in mates:
         _, head, device = at.mate(dy, c)
-        n = dy * 4 + c
-        send(bias_send.at[head], held.at[at.me], b_send.at[n], b_recv.at[n], device)
+        send(bias_send.at[head], held.at[at.me], bias_sent, bias_got, device)
     held[at.me] = bias_send[at.head]
     for name in ("single", "gamma", "beta", "gate", "noised", "query", "key", "value", "cot", "out"):
         loads[name].wait()
@@ -316,33 +324,32 @@
     gamma_v[...] = gamma
     gate_v[...] = gate
     make_acts(noised, cotangent, gamma, beta, gate, w_query, w_key, w_value, w_out, acts_send)
-    send_all_acts(0)
+    for dy, c in MIXED:
+        _, head, device = at.mate(dy, c)
+        send(acts_send.at[head, 0], acts_all.at[at.me, 0], kv_sent, kv_got, device)
     acts_all[at.me] = acts_send[at.head]
-    for dy, c in mates:
-        n = dy * 4 + c
-        arrive(held.at[at.mate(4 - dy, c)[0]], b_send.at[n], b_recv.at[n])
+    arrive(held.at[:15], bias_got)
     bias_all[at.x, at.z] = assemble_bias(held)
     order = (at.z, at.near, at.far, at.opposite)
     rows = bias_all.at[at.x, at.z]
-    send(rows, rows, z_send.at[2], z_recv.at[2], at.same_head(at.far))
-    send(rows, rows, z_send.at[1], z_recv.at[1], at.same_head(at.near))
+    send(rows, rows, z_sent, z_recv.at[1], at.same_head(at.far))
+    send(rows, rows, z_sent, z_recv.at[0], at.same_head(at.near))
     for kz in range(4):
         rows = bias_all.at[at.x, order[kz]]
         if kz:
-            arrive(rows, z_send.at[kz], z_recv.at[kz])
+            arrive(rows, z_recv.at[kz - 1])
         if kz == 2:
-            send(rows, rows, z_send.at[3], z_recv.at[3], at.same_head(at.near))
+            send(rows, rows, z_sent, z_recv.at[2], at.same_head(at.near))
         for k in (2, 1, 3):
-            n = k * 4 + kz
-            send(rows, rows, x_send.at[n], x_recv.at[n], at.along("x", k)[1])
+            send(rows, rows, x_sent, x_recv.at[k], at.along("x", k)[1])
         if kz == 0:
-            send_all_acts(1)
+            for dy, c in MIXED:
+                _, head, device = at.mate(dy, c)
+                source, target = acts_send.at[head, 1], acts_all.at[at.me, 1]
+                send(source, target, q_sent, q_recv.at[dy * 4 + c], device)
+    arrive(acts_all.at[:15, 0], kv_got)
     samples = [(at.y + 4 - dy) % 4 for dy in (1, 2, 3, 0)]
     for s, dy in enumerate((1, 2, 3, 0)):
-        for c in range(4):
-            if dy or c:
-                n = dy * 4 + c
-                arrive(acts_all.at[at.mate(4 - dy, c)[0], 0], a_send.at[n], a_recv.at[n])
         key_t[s] = wide(acts_all, samples[s] * 4, 0)
         value_t[s] = wide(acts_all, samples[s] * 4, 1)
         grad_key[s] = jnp.zeros((HEAD, TOKENS), F32)
@@ -357,17 +364,14 @@
 
         @pl.when(step > 0)
         def _():
-            for kz in range(4):
-                n = (4 - k) * 4 + kz
-                arrive(bias_all.at[place, order[kz]], x_send.at[n], x_recv.at[n])
+            arrive(bias_all.at[place], x_recv.at[4 - k])
 
         @pl.when(c > 0)
         def _():
-            arrive(acts_all.at[at.y * 4 + place, 1], q_send.at[c], q_recv.at[c])
+            arrive(acts_all.at[at.y * 4 + place, 1], q_recv.at[c])
 
         for s, dy in enumerate((1, 2, 3)):
-            n = dy * 4 + c
-            arrive(acts_all.at[samples[s] * 4 + place, 1], q_send.at[n], q_recv.at[n])
+            arrive(acts_all.at[samples[s] * 4 + place, 1], q_recv.at[dy * 4 + c])
         for z in range(4):
             bias_f[z * HEAD : (z + 1) * HEAD, :] = bias_all[place, z].astype(F32) * LOG2E
 
@@ -400,17 +404,15 @@
         def _():
             for kz in (3, 2, 1, 0):
                 z = order[kz]
-                n = k * 4 + kz
-                remote(to_x.at[k, z], from_x.at[at.x, z], u_send.at[n], u_recv.at[n], device).start()
+                send(to_x.at[k, z], from_x.at[at.x, z], u_sent, u_recv.at[kz], device)
 
         for s, dy in enumerate((1, 2, 3, 0)):
             slot = samples[s] * 4 + place
-            n = (4 - dy) % 4 * 4 + c
             copy = remote(
                 grads_send.at[slot, 1],
                 grads_all.at[at.head, 1],
-                o_send.at[n],
-                o_recv.at[n],
+                rows_sent,
+                rows_got,
                 (at.r - at.y + samples[s], place),
             )
             if dy:
@@ -434,28 +436,15 @@
         for c in (2, 0, 3, 1):
             if dy or c:
                 slot, _, device = at.mate(4 - dy, c)
-                n = (4 - dy) % 4 * 4 + c
-                send(
-                    grads_send.at[slot, 0], grads_all.at[at.head, 0], g_send.at[n], g_recv.at[n], device
-                )
-    for dy, c in mates:
-        slot, _, device = at.mate(dy, c)
-        n = dy * 4 + c
-        out.append(
-            remote(grads_send.at[slot, 1], grads_all.at[at.head, 1], o_send.at[n], o_recv.at[n], device)
-        )
-    for k in range(1, 4):
-        for kz in range(4):
-            z = order[kz]
-            n = k * 4 + kz
-            device = at.along("x", k)[1]
-            out.append(remote(to_x.at[k, z], from_x.at[at.x, z], u_send.at[n], u_recv.at[n], device))
+                send(grads_send.at[slot, 0], grads_all.at[at.head, 0], grads_sent, grads_got, device)
     grads_all[at.head] = grads_send[at.me]
     from_x[at.x] = to_x[0]
-
-    for dy, c in mates:
-        n = dy * 4 + c
-        arrive(grads_all.at[at.mate(4 - dy, c)[1], 1], o_send.at[n], o_recv.at[n])
+    left(held.at[:15], bias_sent)
+    left(acts_all.at[:15, 0], kv_sent)
+    left(acts_all.at[:15, 1], q_sent)
+    left(bias_all.at[0, :3], z_sent)
+    left(bias_all.at[:3], x_sent)
+    arrive(grads_all.at[:15, 1], rows_got)
     attended, grad_q = back_pieces(grads_all, 1)
     gamma = gamma_v[...]
     gate = gate_v[...]
@@ -473,89 +462,97 @@
 
     def rows_for(kz):
         z = order[kz]
-        for k in range(1, 4):
-            n = k * 4 + kz
-            arrive(from_x.at[at.along_from("x", k), z], u_send.at[n], u_recv.at[n])
+        arrive(from_x.at[:3, z], u_recv.at[kz])
         rows = from_x[0, z].astype(F32)
         for x in range(1, 4):
             rows = rows + from_x[x, z].astype(F32)
         return rows
 
     to_z[3] = rows_for(3).astype(BF16)
-    send(to_z.at[3], from_z.at[3], z_send.at[7], z_recv.at[7], at.same_head(at.near))
+    send(to_z.at[3], from_z.at[3], near_sent, z_recv.at[5], at.same_head(at.near))
     to_z[1] = rows_for(1).astype(BF16)
-    send(to_z.at[1], from_z.at[1], z_send.at[5], z_recv.at[5], at.same_head(at.near))
-    for dy, c in mates:
-        n = dy * 4 + c
-        arrive(grads_all.at[at.mate(4 - dy, c)[1], 0], g_send.at[n], g_recv.at[n])
+    send(to_z.at[1], from_z.at[1], near_sent, z_recv.at[3], at.same_head(at.near))
+    arrive(grads_all.at[:15, 0], grads_got)
     grad_k, grad_v = back_pieces(grads_all, 0)
     grad_input = inner_v[...] + dot(grad_k, w_key[...], back) + dot(grad_v, w_value[...], back)
     pre_gamma = (grad_input * gamma_v[...]).astype(BF16)
     sums = sums_v[...] + dot(pre_gamma, w_gamma[...], back)
     sums = sums + dot(grad_input.astype(BF16), w_beta[...], back)
-    sums = sums.astype(BF16)
-    for y in range(4):
-        part[y] = sums[y * HEAD : (y + 1) * HEAD]
-    for k in (2, 1, 3):
-        place, device = at.along("y", k)
-        send(part.at[place], sum_y.at[at.y], r_send.at[k], r_recv.at[k], device)
-    sum_y[at.y] = part[at.y]
+    spread = dot(thin_rows(True), sums.astype(BF16)).astype(BF16)
+    for p in range(16):
+        part[p] = spread[p * 16 : (p + 1) * 16]
+    for dx, dy in others:
+        place, device = at.plane(dx, dy)
+        send(part.at[place], plane_in.at[at.spot], plane_sent, plane_got, device)
+    plane_in[at.spot] = part[at.spot]
 
     to_far = rows_for(2)
-    arrive(from_z.at[3], z_send.at[7], z_recv.at[7])
+    arrive(from_z.at[3], z_recv.at[5])
     to_z[2] = (to_far + from_z[3].astype(F32)).astype(BF16)
-    send(to_z.at[2], from_z.at[2], z_send.at[6], z_recv.at[6], at.same_head(at.far))
-    for k in range(1, 4):
-        arrive(sum_y.at[at.along_from("y", k)], r_send.at[k], r_recv.at[k])
-    sum_z[at.z] = total_of(sum_y).astype(BF16)
+    send(to_z.at[2], from_z.at[2], near_sent, z_recv.at[4], at.same_head(at.far))
+    left(grads_all.at[:15, 1], rows_sent)
+    left(grads_all.at[:15, 0], grads_sent)
+    left(from_x.at[:3], u_sent)
+    own_rows = rows_for(0)
+    weight = pair_weight(w_pair_t)
+    shape = (16, BLOCK)
+    mine = iota(shape, 0) + at.spot * ROWS
+    pick = ((iota(shape, 1) == mine) & (iota(shape, 0) < ROWS)).astype(BF16)
+    normed, inverse = norm_rows(dot(pick, single[...]))
+    arrive(plane_in.at[:15], plane_got)
+    total = plane_in[0].astype(F32)
+    for p in range(1, 16):
+        total = total + plane_in[p].astype(F32)
+    sum_z[at.z] = total.astype(BF16)
     for k in (2, 1, 3):
         rows = sum_z.at[at.z]
-        send(rows, rows, r_send.at[4 + k], r_recv.at[4 + k], at.along("z", k)[1])
-    own_rows = rows_for(0)
-    weight = pair_weight(w_pair_t)
-    normed, inverse = norm_rows(single[pl.ds(at.y * HEAD, HEAD), :].astype(F32))
+        send(rows, rows, sum_sent, sum_got, at.along("z", k)[1])
     for kz in (1, 2):
-        arrive(from_z.at[kz], z_send.at[4 + kz], z_recv.at[4 + kz])
+        arrive(from_z.at[kz], z_recv.at[2 + kz])
     own_rows = own_rows + from_z[1].astype(F32) + from_z[2].astype(F32)
     spread_bias((own_rows * TOKENS).astype(BF16), to_group)
     for dy, c in mates:
         slot, _, device = at.mate(dy, c)
-        n = dy * 4 + c
-        send(to_group.at[slot], from_group.at[at.head], h_send.at[n], h_recv.at[n], device)
+        send(to_group.at[slot], from_group.at[at.head], group_sent, group_got, device)
     from_group[at.head] = to_group[at.me]
-    for k in range(1, 4):
-        arrive(sum_z.at[at.along_from("z", k)], r_send.at[4 + k], r_recv.at[4 + k])
-    sum_x[at.x] = total_of(sum_z).astype(BF16)
-    for k in (2, 1, 3):
-        rows = sum_x.at[at.x]
-        send(rows, rows, r_send.at[8 + k], r_recv.at[8 + k], at.along("x", k)[1])
-    for dy, c in mates:
-        n = dy * 4 + c
-        arrive(from_group.at[at.mate(4 - dy, c)[1]], h_send.at[n], h_recv.at[n])
+    arrive(sum_z.at[:3], sum_got)
+    own[...] = norm_back(total_of(sum_z), normed, inverse).astype(BF16)
+    for dx, dy in others:
+        send(own, plane_out.at[at.spot], out_sent, out_got, at.plane(dx, dy)[1])
+    put = pltpu.make_async_copy(own, plane_out.at[at.spot], load.at[2])
+    put.start()
+    arrive(from_group.at[:15], group_got)
     grad_t = jnp.concatenate([from_group[h] for h in range(HEADS)], axis=0)
     grad_t = grad_t.astype(F32).T.astype(BF16)[:BLOCK]
-    pair_back(grad_t, weight, pair, d_pair, range(0, 6))
-    for k in range(1, 4):
-        arrive(sum_x.at[at.along_from("x", k)], r_send.at[8 + k], r_recv.at[8 + k])
-    d_single[at.y] = norm_back(total_of(sum_x), normed, inverse).astype(BF16)
-    for k in (2, 1, 3):
-        rows = d_single.at[at.y]
-        send(rows, rows, r_send.at[12 + k], r_recv.at[12 + k], at.along("y", k)[1])
-    pair_back(grad_t, weight, pair, d_pair, range(6, ROWS))
+    pair_back(grad_t, weight, pair, d_pair, range(ROWS))
     keep = pltpu.make_async_copy(d_pair, d_pair_out, load.at[1])
     keep.start()
+    left(from_z.at[:3], near_sent)
+    left(plane_in.at[:15], plane_sent)
+    left(sum_z.at[:3], sum_sent)
+    left(from_group.at[:15], group_sent)
     save.wait()
     keep.wait()
-    for k in range(1, 4):
-        arrive(d_single.at[at.along_from("y", k)], r_send.at[12 + k], r_recv.at[12 + k])
-    for copy in out:
-        copy.wait_send()
-
-
-def finish_kernel(updated_in, d_single_in, d_pair_in, updated, d_single, d_pair):
-    updated[...] = updated_in[...]
-    d_single[...] = d_single_in[...].astype(F32)
-    d_pair[...] = d_pair_in[...]
+    put.wait()
+    left(plane_in.at[:15], out_sent)
+    arrive(plane_out.at[:15], out_got)
+
+
+def finish_kernel(*refs):
+    sources, results, held, sums, sems = refs[:3], refs[3:6], refs[6:9], refs[9], refs[10]
+    loads = [pltpu.make_async_copy(sources[n], held[n], sems.at[n]) for n in range(3)]
+    ready = (held[0], sums, held[2])
+    stores = [pltpu.make_async_copy(ready[n], results[n], sems.at[3 + n]) for n in range(3)]
+    for copy in loads:
+        copy.start()
+    pick = thin_rows(False)
+    for n in range(3):
+        loads[n].wait()
+        if n == 1:
+            sums[...] = dot(pick, jnp.concatenate([held[1][p] for p in range(16)], axis=0))
+        stores[n].start()
+    for copy in stores:
+        copy.wait()
 
 
 def on_device(
@@ -588,11 +585,11 @@
         block_kernel,
         out_shape=[
             jax.ShapeDtypeStruct((BLOCK, WIDTH), BF16),
-            jax.ShapeDtypeStruct((4, HEAD, half_width), BF16),
+            jax.ShapeDtypeStruct((16, 16, half_width), BF16),
             jax.ShapeDtypeStruct(pair.shape, BF16),
         ],
         in_specs=[ANY] * 15,
-        out_specs=[ANY, VMEM, ANY],
+        out_specs=[ANY] * 3,
         scratch_shapes=[
             space(BLOCK, half_width),
             space(ROWS, BLOCK, 128),
@@ -623,7 +620,12 @@
             space(16, 2, CHUNK, 128),
             space(16, 2, CHUNK, 128),
         ]
-        + [space(4, HEAD, half_width)] * 4
+        + [
+            space(16, 16, half_width),
+            space(16, 16, half_width),
+            space(4, 16, half_width),
+            space(16, half_width),
+        ]
         + [space(BLOCK, WIDTH), space(ROWS, BLOCK, 128)]
         + [wide_space(BLOCK, half_width), wide_space(BLOCK, WIDTH)]
         + [
@@ -632,8 +634,7 @@
             pltpu.SMEM((HEADS,), F32),
             space(HEADS, 128),
         ]
-        + [dma(15)]
-        + [dma(16)] * 20,
+        + [dma(15), dma(13), dma(8), dma(16), dma(4), dma(4), dma(6)],
         compiler_params=pltpu.CompilerParams(
             vmem_limit_bytes=VMEM_BYTES, collective_id=0, has_side_effects=True
         ),
@@ -662,10 +663,18 @@
             jax.ShapeDtypeStruct((BLOCK, half_width), F32),
             jax.ShapeDtypeStruct(pair.shape, BF16),
         ],
-        in_specs=[VMEM] * 3,
-        out_specs=[VMEM] * 3,
+        in_specs=[ANY] * 3,
+        out_specs=[ANY] * 3,
+        scratch_shapes=[
+            space(BLOCK, WIDTH),
+            space(16, 16, half_width),
+            space(*pair.shape),
+            wide_space(BLOCK, half_width),
+            dma(6),
+        ],
+        compiler_params=pltpu.CompilerParams(vmem_limit_bytes=VMEM_BYTES),
         name="finish",
-    )(results[0], results[1].reshape(BLOCK, half_width), results[2])
+    )(*results)
     return updated.reshape(1, BLOCK, WIDTH), d_single, d_pair
 
 

time: 77.8 us -> 71.5 us (0.919)
  Pallas kernels: 75.3 us -> 69.5 us
    pallas_call x1, Pallas kernels: 73 us -> 67.3 us  [on_device(): pl.pallas_call(block_kernel, out_shape=[jax.ShapeDtypeStruct((BLOCK, WIDT...]
where the time goes in v4:
time: 71.5 us; the launch traced here: 71.4 us
  Pallas kernels  69.5 us (97%)
  local copies, waits for them, and re-layouts  1.27 us (2%)
    pallas_call x1, Pallas kernels, on_device(): pl.pallas_call(block_kernel, out_shape=[jax.ShapeDtypeStruct((BLOCK, WIDT...  67.3 us
    pallas_call x1, Pallas kernels, on_device(): pl.pallas_call(finish_kernel, out_shape=[jax.ShapeDtypeStruct((BLOCK, WID...  2.19 us

profile of v4, /device:TPU:2, one launch (start us, length us, event | category | flops | bytes accessed | tf_op | source)
XLA Modules:
  0.0 71.4 jit_solution(6972373817887185529)
XLA Ops:
  0.6 1.3 %reshape.20.cols_in = s32[1,768]{1,0:T(1,128)} reshape(s32[768]{0:T(1024)} %chain_in.1) | data formatting | bytes 6144 | tf_op jit(solution)/shard_map/reshape | solution.py:655
  1.9 67.3 %block.1 = (bf16[192,768]{1,0:T(8,128)(2,1)}, bf16[16,16,384]{2,1,0:T(8,128)(2,1)}, bf16[12,192,128]{2,1,0:T(8,128)(2,1)}) custom-call(bf16[192,384]{1,0:T(8,128)(2,1)} %single_in.1, bf16[12,192,128]{2,1,0:T(8,128)(2,1)} %pair_in.1, bf16[192,768]{1,0:T(8,128)(2,1)} %bitcast.4, bf16[192,768]{1,0:T(8,128)(2,1)} %bitcast.5, bf16[384,768]{1,0:T(8,128)(2,1)} %w_gamma_in.1, ...), custom_call_target="tpu_custom_call" | custom-call | tf_op jit(solution)/shard_map/block/pallas_call | solution.py:584
  69.2 2.2 %finish.1 = (bf16[192,768]{1,0:T(8,128)(2,1)}, f32[192,384]{1,0:T(8,128)}, bf16[12,192,128]{2,1,0:T(8,128)(2,1)}) custom-call(bf16[192,768]{1,0:T(8,128)(2,1)} %get-tuple-element.9.refs_0_, bf16[16,16,384]{2,1,0:T(8,128)(2,1)} %get-tuple-element.10.refs_1_, bf16[12,192,128]{2,1,0:T(8,128)(2,1)} %get-tuple-element.11.refs_2_), custom_call_target="tpu_custom_call" | custom-call | tf_op jit(solution)/shard_map/finish/pallas_call | solution.py:659

commit v5 on v4

--- a/solution.py
+++ b/solution.py
@@ -144,20 +144,12 @@
         bias_send[h, :, 128:] = jnp.concatenate([rows[:, 128:], jnp.zeros((16, 64), BF16)], axis=1)
 
 
-def make_acts(noised, cotangent, gamma, beta, gate, w_query, w_key, w_value, w_out, acts_send):
-    noised_norm, _ = norm_rows(noised[...].astype(F32))
-    x_b = (noised_norm * gamma + beta).astype(BF16)
-    grad_update = (cotangent[...].astype(F32) * gate).astype(BF16)
-    arrays = (
-        (dot(x_b, w_key[...]), dot(x_b, w_value[...])),
-        (dot(x_b, w_query[...]), dot(grad_update, w_out[...], ((1,), (1,)))),
-    )
-    for part, (first, second) in enumerate(arrays):
-        tail = jnp.concatenate([first[128:], second[128:]], axis=0)
-        for n, piece in enumerate((first[:128], second[:128], tail)):
-            piece = piece.T.astype(BF16)
-            for h in range(HEADS):
-                acts_send[h, part, n * HEAD : (n + 1) * HEAD, :] = piece[h * HEAD : (h + 1) * HEAD]
+def put_acts(part, first, second, acts_send):
+    tail = jnp.concatenate([first[128:], second[128:]], axis=0)
+    for n, piece in enumerate((first[:128], second[:128], tail)):
+        piece = piece.T.astype(BF16)
+        for h in range(HEADS):
+            acts_send[h, part, n * HEAD : (n + 1) * HEAD, :] = piece[h * HEAD : (h + 1) * HEAD]
 
 
 def assemble_bias(held):
@@ -276,13 +268,13 @@
             ("single", single_in, single),
             ("gamma", w_gamma_in, w_gamma),
             ("beta", w_beta_in, w_beta),
-            ("gate", w_outgate_in, w_outgate),
             ("noised", noised_in, noised),
-            ("query", w_query_in, w_query),
             ("key", w_key_in, w_key),
             ("value", w_value_in, w_value),
+            ("gate", w_outgate_in, w_outgate),
             ("cot", cotangent_in, cotangent),
             ("out", w_out_in, w_out),
+            ("query", w_query_in, w_query),
         )
     ):
         loads[name] = pltpu.make_async_copy(source, target, load.at[n])
@@ -314,19 +306,29 @@
         _, head, device = at.mate(dy, c)
         send(bias_send.at[head], held.at[at.me], bias_sent, bias_got, device)
     held[at.me] = bias_send[at.head]
-    for name in ("single", "gamma", "beta", "gate", "noised", "query", "key", "value", "cot", "out"):
+    def send_kv(mates):
+        for dy, c in mates:
+            _, head, device = at.mate(dy, c)
+            send(acts_send.at[head, 0], acts_all.at[at.me, 0], kv_sent, kv_got, device)
+
+    for name in ("single", "gamma", "beta", "noised", "key", "value"):
         loads[name].wait()
     single_norm, _ = norm_rows(single[...].astype(F32))
     single_b = single_norm.astype(BF16)
     gamma = jax.nn.sigmoid(dot(single_b, w_gamma[...]))
     beta = dot(single_b, w_beta[...])
+    gamma_v[...] = gamma
+    noised_norm, _ = norm_rows(noised[...].astype(F32))
+    x_b = (noised_norm * gamma + beta).astype(BF16)
+    put_acts(0, dot(x_b, w_key[...]), dot(x_b, w_value[...]), acts_send)
+    send_kv(MIXED[:8])
+    for name in ("gate", "cot", "out", "query"):
+        loads[name].wait()
     gate = jax.nn.sigmoid(dot(single_b, w_outgate[...]))
-    gamma_v[...] = gamma
     gate_v[...] = gate
-    make_acts(noised, cotangent, gamma, beta, gate, w_query, w_key, w_value, w_out, acts_send)
-    for dy, c in MIXED:
-        _, head, device = at.mate(dy, c)
-        send(acts_send.at[head, 0], acts_all.at[at.me, 0], kv_sent, kv_got, device)
+    grad_update = (cotangent[...].astype(F32) * gate).astype(BF16)
+    grad_attn = dot(grad_update, w_out[...], ((1,), (1,)))
+    put_acts(1, dot(x_b, w_query[...]), grad_attn, acts_send)
     acts_all[at.me] = acts_send[at.head]
     arrive(held.at[:15], bias_got)
     bias_all[at.x, at.z] = assemble_bias(held)
@@ -334,6 +336,7 @@
     rows = bias_all.at[at.x, at.z]
     send(rows, rows, z_sent, z_recv.at[1], at.same_head(at.far))
     send(rows, rows, z_sent, z_recv.at[0], at.same_head(at.near))
+    send_kv(MIXED[8:])
     for kz in range(4):
         rows = bias_all.at[at.x, order[kz]]
         if kz:

time: 71.5 us -> 71.2 us (level)
  Pallas kernels: 69.5 us -> 68.5 us
    pallas_call x1, Pallas kernels: 67.3 us -> 66.3 us  [on_device(): pl.pallas_call(block_kernel, out_shape=[jax.ShapeDtypeStruct((BLOCK, WIDT...]
where the time goes in v5:
time: 71.2 us; the launch traced here: 70.4 us
  Pallas kernels  68.5 us (96%)
  local copies, waits for them, and re-layouts  1.27 us (2%)
    pallas_call x1, Pallas kernels, on_device(): pl.pallas_call(block_kernel, out_shape=[jax.ShapeDtypeStruct((BLOCK, WIDT...  66.3 us
    pallas_call x1, Pallas kernels, on_device(): pl.pallas_call(finish_kernel, out_shape=[jax.ShapeDtypeStruct((BLOCK, WID...  2.18 us

profile of v5, /device:TPU:2, one launch (start us, length us, event | category | flops | bytes accessed | tf_op | source)
XLA Modules:
  0.0 70.4 jit_solution(6296197281944046576)
XLA Ops:
  0.6 1.3 %reshape.20.cols_in = s32[1,768]{1,0:T(1,128)} reshape(s32[768]{0:T(1024)} %chain_in.1) | data formatting | bytes 6144 | tf_op jit(solution)/shard_map/reshape | solution.py:658
  1.9 66.3 %block.1 = (bf16[192,768]{1,0:T(8,128)(2,1)}, bf16[16,16,384]{2,1,0:T(8,128)(2,1)}, bf16[12,192,128]{2,1,0:T(8,128)(2,1)}) custom-call(bf16[192,384]{1,0:T(8,128)(2,1)} %single_in.1, bf16[12,192,128]{2,1,0:T(8,128)(2,1)} %pair_in.1, bf16[192,768]{1,0:T(8,128)(2,1)} %bitcast.4, bf16[192,768]{1,0:T(8,128)(2,1)} %bitcast.5, bf16[384,768]{1,0:T(8,128)(2,1)} %w_gamma_in.1, ...), custom_call_target="tpu_custom_call" | custom-call | tf_op jit(solution)/shard_map/block/pallas_call | solution.py:587
  68.2 2.2 %finish.1 = (bf16[192,768]{1,0:T(8,128)(2,1)}, f32[192,384]{1,0:T(8,128)}, bf16[12,192,128]{2,1,0:T(8,128)(2,1)}) custom-call(bf16[192,768]{1,0:T(8,128)(2,1)} %get-tuple-element.9.refs_0_, bf16[16,16,384]{2,1,0:T(8,128)(2,1)} %get-tuple-element.10.refs_1_, bf16[12,192,128]{2,1,0:T(8,128)(2,1)} %get-tuple-element.11.refs_2_), custom_call_target="tpu_custom_call" | custom-call | tf_op jit(solution)/shard_map/finish/pallas_call | solution.py:662

commit v6 on v5

--- a/solution.py
+++ b/solution.py
@@ -343,7 +343,7 @@
             arrive(rows, z_recv.at[kz - 1])
         if kz == 2:
             send(rows, rows, z_sent, z_recv.at[2], at.same_head(at.near))
-        for k in (2, 1, 3):
+        for k in (1, 3, 2):
             send(rows, rows, x_sent, x_recv.at[k], at.along("x", k)[1])
         if kz == 0:
             for dy, c in MIXED:

time: 71.2 us -> 70.5 us (level)
  no operation moved by 1% of the time
where the time goes in v6:
time: 70.5 us; the launch traced here: 69.8 us
  Pallas kernels  67.9 us (96%)
  local copies, waits for them, and re-layouts  1.27 us (2%)
    pallas_call x1, Pallas kernels, on_device(): pl.pallas_call(block_kernel, out_shape=[jax.ShapeDtypeStruct((BLOCK, WIDT...  65.7 us
    pallas_call x1, Pallas kernels, on_device(): pl.pallas_call(finish_kernel, out_shape=[jax.ShapeDtypeStruct((BLOCK, WID...  2.18 us

profile of v6, /device:TPU:2, one launch (start us, length us, event | category | flops | bytes accessed | tf_op | source)
XLA Modules:
  0.0 69.8 jit_solution(1411466872158849759)
XLA Ops:
  0.6 1.3 %reshape.20.cols_in = s32[1,768]{1,0:T(1,128)} reshape(s32[768]{0:T(1024)} %chain_in.1) | data formatting | bytes 6144 | tf_op jit(solution)/shard_map/reshape | solution.py:658
  1.9 65.7 %block.1 = (bf16[192,768]{1,0:T(8,128)(2,1)}, bf16[16,16,384]{2,1,0:T(8,128)(2,1)}, bf16[12,192,128]{2,1,0:T(8,128)(2,1)}) custom-call(bf16[192,384]{1,0:T(8,128)(2,1)} %single_in.1, bf16[12,192,128]{2,1,0:T(8,128)(2,1)} %pair_in.1, bf16[192,768]{1,0:T(8,128)(2,1)} %bitcast.4, bf16[192,768]{1,0:T(8,128)(2,1)} %bitcast.5, bf16[384,768]{1,0:T(8,128)(2,1)} %w_gamma_in.1, ...), custom_call_target="tpu_custom_call" | custom-call | tf_op jit(solution)/shard_map/block/pallas_call | solution.py:587
  67.6 2.2 %finish.1 = (bf16[192,768]{1,0:T(8,128)(2,1)}, f32[192,384]{1,0:T(8,128)}, bf16[12,192,128]{2,1,0:T(8,128)(2,1)}) custom-call(bf16[192,768]{1,0:T(8,128)(2,1)} %get-tuple-element.9.refs_0_, bf16[16,16,384]{2,1,0:T(8,128)(2,1)} %get-tuple-element.10.refs_1_, bf16[12,192,128]{2,1,0:T(8,128)(2,1)} %get-tuple-element.11.refs_2_), custom_call_target="tpu_custom_call" | custom-call | tf_op jit(solution)/shard_map/finish/pallas_call | solution.py:662
